TPU v7x, 32 devices: a whole 2x2x4 slice. The times are simulated.
32 devices in a mesh: rows: 4 (over y, x), tm: 8 (over z, core).
Axes of the slice: x: 2, y: 2, z: 4, core: 2. Of those that a mesh axis runs over, the one named last changes fastest.
Arguments:
- frames: bfloat16 [4, 4, 1024, 512], P(None, 'rows', 'tm'), may hold values from -6 to 6
- segment_ids: int32 [4, 4, 1024], P(None, 'rows', 'tm'), may hold values from 0 to 16, as said below
- norm_gains: float32 [2, 5, 512], replicated, may hold values from 0.5 to 1.5
- feed_in: bfloat16 [2, 2, 512, 2048], replicated, may hold values from -0.25 to 0.25
- feed_out: bfloat16 [2, 2, 2048, 512], replicated, may hold values from -0.125 to 0.125
- attend_in: bfloat16 [2, 512, 1536], replicated, may hold values from -0.25 to 0.25
- attend_out: bfloat16 [2, 512, 512], replicated, may hold values from -1.5 to 1.5
- point_in: bfloat16 [2, 512, 1024], replicated, may hold values from -0.25 to 0.25
- depthwise: float32 [2, 9, 512], replicated, may hold values from -2 to 2
- stat_mean: float32 [2, 512], replicated, may hold values from -1.75 to 1.75
- stat_var: float32 [2, 512], replicated, may hold values from 0.2 to 2
- batch_scale: float32 [2, 512], replicated, may hold values from 0.5 to 1.5
- batch_shift: float32 [2, 512], replicated, may hold values from -1.75 to 1.75
- point_out: bfloat16 [2, 512, 512], replicated, may hold values from -0.25 to 0.25
- cotangent: bfloat16 [4, 4, 1024, 512], P(None, 'rows', 'tm'), may hold values from -6 to 6
Outputs:
- activations: bfloat16 [4, 4, 1024, 512], P(None, 'rows', 'tm')
- frames_grad: bfloat16 [4, 4, 1024, 512], P(None, 'rows', 'tm')
- gains_grad: float32 [2, 5, 512], P(None, None, 'tm')
- feed_in_grad: float32 [2, 2, 512, 2048], P(None, None, None, 'tm')
- feed_out_grad: float32 [2, 2, 2048, 512], P(None, None, None, 'tm')
- attend_in_grad: float32 [2, 512, 1536], P(None, None, 'tm')
- attend_out_grad: float32 [2, 512, 512], P(None, None, 'tm')
- point_in_grad: float32 [2, 512, 1024], P(None, None, 'tm')
- depthwise_grad: float32 [2, 9, 512], P(None, None, 'tm')
- scale_grad: float32 [2, 512], P(None, 'tm')
- shift_grad: float32 [2, 512], P(None, 'tm')
- point_out_grad: float32 [2, 512, 512], P(None, None, 'tm')
Inputs may be any that keep to these rules, and one draw needn't show every extreme that they name: `segment_ids`: along each row the ids never fall and rise by one at a time; every utterance is shorter than 128 frames and lies within two adjacent blocks of 128 frames (frames j * 128 to (j + 2) * 128 - 1 for some j); every boundary between two blocks is crossed by an utterance.
All inputs are finite; a program needn't handle non-finite values.
Results may differ from a plain program's by a relative error of at most 0.023.
Values may be sent and summed in bfloat16 or wider, within the bound.
No kernel may reach another device: no remote copies, remote signals or barrier semaphores. Data moves between devices by JAX's collectives and lax.ppermute only.
A program may use at most 384 MiB of HBM per device.

v0:
```python
import functools

import jax
import jax.numpy as jnp
import numpy as np
from jax import lax
from jax.experimental import pallas as pl
from jax.experimental.pallas import tpu as pltpu
from jax.sharding import PartitionSpec as P

HD = 64
KERNEL = 9
HALO = 4
EPSILON = 1e-05
MASKED = -1e30
BF = jnp.bfloat16
F32 = jnp.float32
D = 512
FF = 2048
BLK = 128
ROW_CHOICES = (640, 1024)
CAP = ROW_CHOICES[-1]
LANES = 256
SMALL_ROWS = 128
TAIL_WORK = 3e10
PAIRS = D // 128
VMEM_LIMIT = 60 * 2**20
VMEM_SMALL = 24 * 2**20
ANY = pl.BlockSpec(memory_space=pl.ANY)
VMEM = pl.BlockSpec(memory_space=pltpu.VMEM)
SMEM = pl.BlockSpec(memory_space=pltpu.SMEM)


def shifted(array, axis, by):
    size = lax.axis_size(axis)
    pairs = [(i, i + by) for i in range(size) if 0 <= i + by < size]
    return lax.ppermute(array, axis, pairs)


def struct(shape, dtype):
    return jax.ShapeDtypeStruct(shape, dtype)


def call(body, ins, outs, scratch, args, flops=0, moved=0, name="kernel", deps=(), vmem=VMEM_LIMIT):
    count = len(ins)

    def inner(*refs):
        body(*refs[:count], *refs[count + len(deps) :])

    return pl.pallas_call(
        inner,
        out_shape=[s for s, _ in outs],
        in_specs=list(ins) + [ANY] * len(deps),
        out_specs=[b for _, b in outs],
        scratch_shapes=scratch,
        compiler_params=pltpu.CompilerParams(vmem_limit_bytes=vmem),
        cost_estimate=pl.CostEstimate(flops=int(flops), bytes_accessed=int(moved), transcendentals=0),
        name=name,
    )(*args, *deps)


def dot_nn(a, b):
    return jnp.dot(a, b, preferred_element_type=F32)


def dot_nt(a, b):
    return lax.dot_general(a, b, (((1,), (1,)), ((), ())), preferred_element_type=F32)


def dot_tn(a, b):
    return lax.dot_general(a, b, (((0,), (0,)), ((), ())), preferred_element_type=F32)


def sigmoid(v):
    return 0.5 + 0.5 * jnp.tanh(0.5 * v)


def normalise(x):
    c = x - jnp.mean(x, axis=-1, keepdims=True)
    inv = lax.rsqrt(jnp.mean(c * c, axis=-1, keepdims=True) + EPSILON)
    return c * inv, inv


def norm_back(grad, xhat, inv, gain):
    w = grad * gain
    return inv * (
        w - jnp.mean(w, axis=-1, keepdims=True) - xhat * jnp.mean(w * xhat, axis=-1, keepdims=True)
    )


def fold(v):
    return jnp.sum(v.reshape(v.shape[0] // 8, 8, v.shape[1]), axis=0)


def total(v):
    return jnp.sum(v, axis=0, keepdims=True)


def by_rows(n_ref, body):
    low = 0
    for rows in ROW_CHOICES:
        n = n_ref[0]
        cond = n > low
        if rows != CAP:
            cond = cond & (n <= rows)

        @pl.when(cond)
        def _(rows=rows):
            body(rows)

        low = rows


def blocks(rows, step, init=None, size=128):
    def wrapped(i, carry):
        at = pl.ds(pl.multiple_of(i * size, size), size)
        return step(i, at, carry)

    start = init if init is not None else jnp.int32(0)
    return lax.fori_loop(0, rows // size, wrapped, start, unroll=rows == ROW_CHOICES[0])


def each(count, rows, step):
    if rows == ROW_CHOICES[0]:
        for i in range(count):
            step(i)
    else:

        def wrapped(i, carry):
            step(i)
            return carry

        lax.fori_loop(0, count, wrapped, jnp.int32(0))


def cut(i, size):
    return pl.ds(i * size, size) if isinstance(i, int) else pl.ds(pl.multiple_of(i * size, size), size)


def rope_tables():
    half = HD // 2
    freq = np.power(np.float32(10000.0), -(np.arange(half).astype(np.float32) / np.float32(half)))
    angle = np.arange(BLK).astype(np.float32)[:, None] * freq.astype(np.float32)[None, :]
    cos = np.cos(angle.astype(np.float64))
    sin = np.sin(angle.astype(np.float64))
    full = (np.concatenate([cos] * 4, axis=1), np.concatenate([-sin, sin] * 2, axis=1))
    parts = []
    for table in full:
        rest = table
        for _ in range(3):
            piece = rest.astype(jnp.bfloat16)
            parts.append(piece)
            rest = rest - piece.astype(np.float64)
    return np.stack(parts)


def pack_body(
    ids_ref, frames_ref, cot_ref, below_ref, above_ref, tab_ref,
    x_ref, g_ref, p_ref, cos_ref, sin_ref, kb_ref, kr_ref, n_ref,
    keep_s, key_s, dest_s, pos_s, win_s, cot_s,
):
    batches = ids_ref.shape[0]
    half = batches // 2
    shown = (8, BLK)
    below_ids = below_ref[pl.ds(4 * BLK, 16), :].astype(F32)[0:1]
    above_ids = above_ref[pl.ds(4 * BLK, 16), :].astype(F32)[0:1]
    for m in range(batches):
        own = ids_ref[m : m + 1, :]
        below = below_ids[:, m * BLK : (m + 1) * BLK]
        above = above_ids[:, m * BLK : (m + 1) * BLK]
        i = m // 2
        mine = pl.ds(m * BLK, BLK)
        theirs = (pl.ds(i * BLK, BLK), pl.ds((half + i) * BLK, BLK))
        if m % 2 == 0:
            pieces = ((own, own != below[:, BLK - 1 : BLK]), (above, above == own[:, BLK - 1 : BLK]))
            frames = ((frames_ref, mine, cot_ref, mine), (above_ref, theirs[0], above_ref, theirs[1]))
        else:
            pieces = ((below, below == own[:, 0:1]), (own, own != above[:, 0:1]))
            frames = ((below_ref, theirs[0], below_ref, theirs[1]), (frames_ref, mine, cot_ref, mine))
        for j in range(2):
            at = pl.ds((2 * m + j) * BLK, BLK)
            key_s[:, at] = jnp.broadcast_to(pieces[j][0] + 4096.0 * m, shown)
            keep_s[:, at] = jnp.broadcast_to(jnp.where(pieces[j][1], 1.0, 0.0), shown)
            src, rows, cot, cot_rows = frames[j]
            win_s[at, :] = src[rows, :]
            cot_s[at, :] = cot[cot_rows, :]
    square = (BLK, BLK)
    earlier = lax.broadcasted_iota(jnp.int32, square, 0) < lax.broadcasted_iota(jnp.int32, square, 1)
    ramp = earlier.astype(F32).astype(BF)
    before = jnp.zeros((8, 1), F32)
    for j in range(2 * batches):
        at = pl.ds(j * BLK, BLK)
        keep = keep_s[:, at]
        dest_s[:, at] = jnp.where(keep > 0.5, before + dot_nn(keep.astype(BF), ramp), -1.0)
        before = before + jnp.sum(keep, axis=1, keepdims=True)
    n = (jnp.sum(before) * 0.125 + 0.5).astype(jnp.int32)
    n_ref[0] = n
    for m in range(batches):
        first, second = pl.ds(2 * m * BLK, BLK), pl.ds((2 * m + 1) * BLK, BLK)
        cols = [jnp.broadcast_to(key_s[0:1, at], square).T for at in (first, second)]
        count = lambda mask: jnp.broadcast_to(jnp.sum(jnp.where(mask, 1.0, 0.0), axis=0, keepdims=True), shown)
        pos_s[:, first] = count((cols[0] == key_s[0:1, first]) & earlier)
        pos_s[:, second] = count(cols[0] == key_s[0:1, second]) + count((cols[1] == key_s[0:1, second]) & earlier)
    kr_ref[...] = jnp.full(kr_ref.shape, -1.0, F32)
    rows_all = 2 * batches * BLK

    def step(i, at):
        row = (lax.broadcasted_iota(jnp.int32, (BLK, rows_all), 0) + i * BLK).astype(F32)
        pick = jnp.where(dest_s[0:1, :] == row, 1.0, 0.0)
        p = pick.astype(BF)
        p_ref[at, :] = p
        x_ref[at, :] = dot_nn(p, win_s[...])
        g_ref[at, :] = dot_nn(p, cot_s[...])
        key = jnp.broadcast_to(jnp.sum(pick * key_s[0:1, :], axis=1, keepdims=True), square)
        kb_ref[at, :] = key
        kr_ref[:, pl.ds(i * BLK + BLK, BLK)] = key.T[0:8]
        pos = jnp.sum(pick * pos_s[0:1, :], axis=1, keepdims=True)
        hot = (lax.broadcasted_iota(jnp.int32, square, 1).astype(F32) == pos).astype(F32).astype(BF)
        cos_ref[at, :] = dot_nn(hot, tab_ref[0]) + dot_nn(hot, tab_ref[1]) + dot_nn(hot, tab_ref[2])
        sin_ref[at, :] = dot_nn(hot, tab_ref[3]) + dot_nn(hot, tab_ref[4]) + dot_nn(hot, tab_ref[5])

    for i in range(rows_all // BLK):
        at = pl.ds(i * BLK, BLK)
        if i * BLK < ROW_CHOICES[0]:
            step(i, at)
        else:

            @pl.when(n > ROW_CHOICES[0])
            def _(i=i, at=at):
                step(i, at)

            @pl.when(n <= ROW_CHOICES[0])
            def _(at=at):
                p_ref[at, :] = jnp.zeros((BLK, rows_all), BF)


def pack(ids, frames, cotangent, below, above):
    vm = pltpu.VMEM
    return call(
        pack_body,
        [VMEM] * 6,
        [
            (struct((CAP, D), F32), VMEM),
            (struct((CAP, D), F32), VMEM),
            (struct((CAP, CAP), BF), VMEM),
            (struct((CAP, 128), F32), VMEM),
            (struct((CAP, 128), F32), VMEM),
            (struct((CAP, 128), F32), VMEM),
            (struct((8, CAP + 2 * BLK), F32), VMEM),
            (struct((1,), jnp.int32), SMEM),
        ],
        [vm((8, CAP), F32), vm((8, CAP), F32), vm((8, CAP), F32), vm((8, CAP), F32), vm((CAP, D), BF), vm((CAP, D), BF)],
        (ids, frames, cotangent, below, above, jnp.asarray(rope_tables(), dtype=BF)),
        flops=4 * CAP * CAP * D,
        moved=12 * 2**20,
        name="pack",
    )


def lane_low(shape):
    return lax.broadcasted_iota(jnp.int32, shape, 1) % HD < HD // 2


def swap_halves(v):
    return jnp.where(lane_low(v.shape), pltpu.roll(v, 128 - HD // 2, 1), pltpu.roll(v, HD // 2, 1))


def stacked(v):
    first = lax.broadcasted_iota(jnp.int32, v.shape, 1) < HD
    zero = jnp.zeros_like(v)
    return jnp.concatenate([jnp.where(first, v, zero), jnp.where(first, zero, v)], axis=0)


def unstacked(v):
    half = v.shape[0] // 2
    first = lax.broadcasted_iota(jnp.int32, (half, 128), 1) < HD
    return jnp.where(first, v[:half], v[half:])


def norm_into(x_ref, gain, a_ref, rows):
    def step(i, at, carry):
        xhat, _ = normalise(x_ref[at, :])
        a_ref[at, :] = (xhat * gain).astype(BF)
        return carry

    blocks(rows, step)


def forward_body(
    n_ref, x0_ref, cos_ref, sin_ref, kb_ref, kr_ref, gains_ref, taps_ref, mean_ref, var_ref, scale_ref, shift_ref,
    fin_h, fout_h, ain_h, aout_h, pin_h, pout_h,
    act_ref, xs_h, hs_h, q_h, kv_h, at_h, o_h, u_h, z_h,
    fin, fout, ain, aout, pin, pout, xb, hb, qb, kvb, ab, ob, ub, zb, a_s, gp, kp, w_sem, s_sem,
):
    layers = gains_ref.shape[0]
    weights = [
        (fin_h, (0,), fin.at[0]), (fout_h, (0,), fout.at[0]), (ain_h, (), ain), (aout_h, (), aout),
        (pin_h, (), pin), (pout_h, (), pout), (fin_h, (1,), fin.at[1]), (fout_h, (1,), fout.at[1]),
    ]

    def weight_copy(i, l):
        src, sub, dst = weights[i]
        return pltpu.make_async_copy(src.at[(l,) + sub], dst, w_sem.at[i])

    for i in (0, 1):
        weight_copy(i, 0).start()

    def run(rows):
        tiles = rows // BLK
        top = pl.ds(0, rows)
        saves = [(xb.at[i, top], lambda l, i=i: xs_h.at[l, i, top]) for i in range(5)]
        saves += [(hb.at[k, top], lambda l, k=k: hs_h.at[l, k, top]) for k in range(2)]
        saves += [
            (qb.at[top], lambda l: q_h.at[l, top]),
            (kvb.at[pl.ds(0, rows + 2 * BLK)], lambda l: kv_h.at[l, pl.ds(0, rows + 2 * BLK)]),
            (ab.at[pl.ds(0, tiles)], lambda l: at_h.at[l, pl.ds(0, tiles)]),
            (ob.at[top], lambda l: o_h.at[l, top]),
            (ub.at[top], lambda l: u_h.at[l, top]),
            (zb.at[top], lambda l: z_h.at[l, top]),
        ]

        def save(i, l):
            src, dst = saves[i]
            return pltpu.make_async_copy(src, dst(l), s_sem.at[i])

        def settle(i, l):
            @pl.when(l > 0)
            def _():
                save(i, l - 1).wait()

        def use(i, l):
            weight_copy(i, l).wait()

        def next_weight(i, l):
            @pl.when(l + 1 < layers)
            def _():
                weight_copy(i, l + 1).start()

        kvb[pl.ds(0, BLK), :] = jnp.zeros((BLK, 2 * D), BF)
        kvb[pl.ds(rows + BLK, BLK), :] = jnp.zeros((BLK, 2 * D), BF)
        gp[:, pl.ds(0, 8), :] = jnp.zeros((PAIRS, 8, 128), F32)
        gp[:, pl.ds(rows + 8, 8), :] = jnp.zeros((PAIRS, 8, 128), F32)
        kp[pl.ds(0, BLK), :] = jnp.full((BLK, 128), -1.0, F32)
        kp[pl.ds(rows + BLK, BLK), :] = jnp.full((BLK, 128), -1.0, F32)

        def fill(i, at, carry):
            kp[pl.ds(pl.multiple_of(i * BLK + BLK, BLK), BLK), :] = kb_ref[at, :]
            xb[0, at, :] = x0_ref[at, :]
            return carry

        blocks(rows, fill)

        def feed(l, k, src, dst, gain, wi, early=lambda: None):
            settle(5 + k, l)
            settle(dst, l)

            def first(i, at, carry):
                x = xb[src, at, :]
                xhat, _ = normalise(x)
                a_s[at, :] = (xhat * gain).astype(BF)
                xb[dst, at, :] = x
                return carry

            blocks(rows, first)
            use(wi, l)
            use(wi + 1, l)
            early()

            def chunk(c):
                cols = cut(c, 512)
                h = dot_nn(a_s[top, :], fin[k, :, cols])
                hb[k, top, cols] = h.astype(BF)
                s = (h * sigmoid(h)).astype(BF)
                xb[dst, top, :] = xb[dst, top, :] + 0.5 * dot_nn(s, fout[k, cols, :])

            each(FF // 512, rows, chunk)
            next_weight(wi, l)
            next_weight(wi + 1, l)
            save(5 + k, l).start()
            save(dst, l).start()

        def first_weights(l, which):
            @pl.when(l == 0)
            def _():
                for i in which:
                    weight_copy(i, 0).start()

        def layer(l, carry):
            gains = [gains_ref[l, pl.ds(i, 1), :] for i in range(5)]
            save(0, l).start()
            feed(l, 0, 0, 1, gains[0], 0, lambda: first_weights(l, (2, 3)))
            first_weights(l, (4, 5, 6, 7))

            norm_into(xb.at[1], gains[1], a_s, rows)
            settle(7, l)
            settle(8, l)
            settle(9, l)
            settle(10, l)
            use(2, l)
            for part in range(3):
                proj = dot_nn(a_s[top, :], ain[:, part * D : (part + 1) * D])
                for p in range(PAIRS):
                    lanes = slice(p * 128, (p + 1) * 128)
                    v = proj[:, lanes]
                    if part < 2:
                        v = v * cos_ref[top, :] + swap_halves(v) * sin_ref[top, :]
                    if part == 0:
                        qb[top, lanes] = (v * HD**-0.5).astype(BF)
                    elif part == 1:
                        kvb[pl.ds(BLK, rows), lanes] = v.astype(BF)
                    else:
                        kvb[pl.ds(BLK, rows), D + p * 128 : D + (p + 1) * 128] = v.astype(BF)
            next_weight(2, l)

            def tile(t, at, c):
                near = pl.ds(pl.multiple_of(t * BLK, BLK), 3 * BLK)
                same = kp[near, :] == kr_ref[0:1, pl.ds(pl.multiple_of(t * BLK + BLK, BLK), BLK)]
                same = jnp.concatenate([same, same], axis=1)
                for p in range(PAIRS):
                    lanes = slice(p * 128, (p + 1) * 128)
                    s = dot_nt(kvb[near, lanes], stacked(qb[at, lanes]))
                    s = jnp.where(same, s, MASKED)
                    e = jnp.exp(s - jnp.max(s, axis=0, keepdims=True))
                    low = (e * (1.0 / jnp.sum(e, axis=0, keepdims=True))).astype(BF)
                    ab[t, p] = low
                    o = dot_tn(low, kvb[near, D + p * 128 : D + (p + 1) * 128])
                    ob[at, lanes] = unstacked(o).astype(BF)
                return c

            blocks(rows, tile)
            settle(2, l)
            use(3, l)
            xb[2, top, :] = xb[1, top, :] + dot_nn(ob[top, :], aout[...])
            next_weight(3, l)
            for i in (7, 8, 9, 10, 2):
                save(i, l).start()

            norm_into(xb.at[2], gains[2], a_s, rows)
            settle(11, l)
            settle(12, l)
            use(4, l)
            for half in range(2):
                lanes = slice(half * 256, (half + 1) * 256)
                up1 = dot_nn(a_s[top, :], pin[:, half * 256 : (half + 1) * 256])
                up2 = dot_nn(a_s[top, :], pin[:, D + half * 256 : D + (half + 1) * 256])
                ub[top, lanes] = up1.astype(BF)
                ub[top, D + half * 256 : D + (half + 1) * 256] = up2.astype(BF)
                gated = (up1 * sigmoid(up2)).astype(BF).astype(F32)
                for q in range(2):
                    gp[2 * half + q, pl.ds(8, rows), :] = gated[:, q * 128 : (q + 1) * 128]
            next_weight(4, l)
            rs = lax.rsqrt(var_ref[pl.ds(l, 1), :] + EPSILON)
            mean = mean_ref[pl.ds(l, 1), :]
            scale = scale_ref[pl.ds(l, 1), :]
            shift = shift_ref[pl.ds(l, 1), :]

            def conv(t, at, c):
                near = [pl.ds(t * BLK + 4 + o, BLK) for o in range(KERNEL)]
                own = kb_ref[at, :]
                masks = [kp[pl.ds(t * BLK + BLK - HALO + o, BLK), :] == own for o in range(KERNEL)]
                for p in range(PAIRS):
                    lanes = slice(p * 128, (p + 1) * 128)
                    z = jnp.zeros((BLK, 128), F32)
                    for o in range(KERNEL):
                        w = taps_ref[l, o : o + 1, lanes]
                        z = z + jnp.where(masks[o], w * gp[p, near[o], :], 0.0)
                    zb[at, lanes] = z
                    b = (z - mean[:, lanes]) * rs[:, lanes] * scale[:, lanes] + shift[:, lanes]
                    a_s[at, lanes] = (b * sigmoid(b)).astype(BF)
                return c

            blocks(rows, conv)
            settle(3, l)
            use(5, l)
            xb[3, top, :] = xb[2, top, :] + dot_nn(a_s[top, :], pout[...])
            next_weight(5, l)
            for i in (11, 12, 3):
                save(i, l).start()

            feed(l, 1, 3, 4, gains[3], 6)
            save(0, l).wait()

            def last(i, at, c):
                xhat, _ = normalise(xb[4, at, :])
                y = xhat * gains[4]
                xb[0, at, :] = y
                act_ref[at, :] = y.astype(BF)
                return c

            blocks(rows, last)
            return carry

        lax.fori_loop(0, layers, layer, jnp.int32(0))
        for i in range(1, len(saves)):
            save(i, layers - 1).wait()
        if rows < CAP:
            act_ref[pl.ds(rows, CAP - rows), :] = jnp.zeros((CAP - rows, D), BF)

    by_rows(n_ref, run)


def forward(n, x0, cos, sin, kb, kr, small, mats):
    layers = small[0].shape[0]
    outs = [
        (struct((CAP, D), BF), VMEM),
        (struct((layers, 5, CAP, D), F32), ANY),
        (struct((layers, 2, CAP, FF), BF), ANY),
        (struct((layers, CAP, D), BF), ANY),
        (struct((layers, CAP + 2 * BLK, 2 * D), BF), ANY),
        (struct((layers, CAP // BLK, PAIRS, 3 * BLK, 2 * BLK), BF), ANY),
        (struct((layers, CAP, D), BF), ANY),
        (struct((layers, CAP, 2 * D), BF), ANY),
        (struct((layers, CAP, D), F32), ANY),
    ]
    vm = pltpu.VMEM
    scratch = [
        vm((2, D, FF), BF), vm((2, FF, D), BF), vm((D, 3 * D), BF), vm((D, D), BF), vm((D, 2 * D), BF), vm((D, D), BF),
        vm((5, CAP, D), F32), vm((2, CAP, FF), BF), vm((CAP, D), BF), vm((CAP + 2 * BLK, 2 * D), BF),
        vm((CAP // BLK, PAIRS, 3 * BLK, 2 * BLK), BF), vm((CAP, D), BF), vm((CAP, 2 * D), BF), vm((CAP, D), F32),
        vm((CAP, D), BF), vm((PAIRS, CAP + 16, 128), F32), vm((CAP + 2 * BLK, 128), F32),
        pltpu.SemaphoreType.DMA((8,)), pltpu.SemaphoreType.DMA((13,)),
    ]
    return call(
        forward_body,
        [SMEM] + [VMEM] * 11 + [ANY] * 6,
        outs,
        scratch,
        (n, x0, cos, sin, kb, kr, *small, *mats),
        flops=2 * 640 * 12e6,
        moved=60 * 2**20,
        name="forward",
    )


class Out:
    def __init__(self, core, buf, kept_h, sent_h, sem):
        self.core = core
        self.buf = buf
        self.homes = (kept_h, sent_h)
        self.sem = sem

    def put(self, at, pair):
        self.buf[(self.core,) + at] = pair[0].astype(BF)
        self.buf[(1 - self.core,) + at] = pair[1].astype(BF)

    def copies(self, slot, at):
        return [
            pltpu.make_async_copy(self.buf.at[(i,) + at], home.at[at], self.sem.at[2 * slot + i])
            for i, home in enumerate(self.homes)
        ]

    def send(self, slot, at):
        for c in self.copies(slot, at):
            c.start()

    def wait(self, slot, at):
        for c in self.copies(slot, at):
            c.wait()


def transposed_out(out, dwo, first):
    for z in range(4):
        for b in range(dwo.shape[1] // LANES):
            pair = [dwo[z * 128 + q * 64 : z * 128 + q * 64 + 64, b * LANES : (b + 1) * LANES] for q in range(2)]
            out.put((z, first(b), slice(None)), pair)


def feed_part(l, k, what, core_ref, g_s, ins, outs, scratch):
    final = k == 1
    do_out, do_in = what != "in", what != "out"
    base = D if do_in else 0
    gains_ref, xs_h, hs_h, fin_h, fout_h, *small_refs = ins
    others = len(small_refs)
    keep_h, send_h, small_ref = outs
    x_s, x4_s, h_s, fin, fout, gl_s, a_s, da_s, buf, sem, osem = scratch
    gain = gains_ref[l, pl.ds(3 if final else 0, 1), :]
    gain4 = gains_ref[l, pl.ds(4, 1), :]
    out = Out(core_ref[0], buf, keep_h, send_h, osem)
    every = pl.ds(0, 4)
    high = base + FF * D // (8 * LANES) if do_out else D

    def run(rows):
        top = pl.ds(0, rows)

        def chunk_in(c):
            cols = cut(c, 512)
            made = [pltpu.make_async_copy(hs_h.at[l, k, top, cols], h_s.at[top, cols], sem.at[3 + 3 * c])]
            if do_in:
                made += [
                    pltpu.make_async_copy(fout_h.at[l, k, cols], fout.at[cols], sem.at[4 + 3 * c]),
                    pltpu.make_async_copy(fin_h.at[l, k, :, cols], fin.at[:, cols], sem.at[5 + 3 * c]),
                ]
            return made

        starts = []
        if do_in:
            starts.append(pltpu.make_async_copy(xs_h.at[l, 3 if final else 0, top], x_s.at[top], sem.at[1]))
        if final:
            starts.insert(0, pltpu.make_async_copy(xs_h.at[l, 4, top], x4_s.at[top], sem.at[2]))

        def start():
            for c in starts + chunk_in(0):
                c.start()

        def first(i, at, carry):
            g = g_s[at, :]
            if final:
                xhat, inv = normalise(x4_s[at, :])
                carry = carry + fold(g * xhat)
                g = norm_back(g, xhat, inv, gain4)
                g_s[at, :] = g
            gl_s[at, :] = (0.5 * g).astype(BF)
            if do_in:
                xhat, _ = normalise(x_s[at, :])
                a_s[at, :] = (xhat * gain).astype(BF)
                da_s[at, :] = jnp.zeros((BLK, D), F32)
            return carry

        def low_rows(c):
            low = base + c * 128
            return pl.ds(low, 128) if isinstance(c, int) else pl.ds(pl.multiple_of(low, 128), 128)

        def spots(c):
            return [(c, pl.ds(0, D))] * do_in + [(every, low_rows(c))] * do_out

        def chunk(c):
            cols = cut(c, 512)
            for copy in chunk_in(c):
                copy.wait()
            if isinstance(c, int):
                for copy in chunk_in(c + 2) if c < 2 else []:
                    copy.start()
            else:

                @pl.when(c < 2)
                def _():
                    for copy in chunk_in(c + 2):
                        copy.start()

            h = h_s[top, cols].astype(F32)
            sig = sigmoid(h)
            if do_in:
                ds = dot_nt(gl_s[top, :], fout[cols, :])
                dh = (ds * (sig * (1.0 + h * (1.0 - sig)))).astype(BF)
                dwi = dot_tn(a_s[top, :], dh)
                out.put((c, pl.ds(0, D), slice(None)), (dwi[:, :LANES], dwi[:, LANES:]))
            if do_out:
                dwo = dot_tn(gl_s[top, :], (h * sig).astype(BF))
                step = lambda b: (base + (2 * c + b) * 64)
                transposed_out(
                    out, dwo,
                    lambda b: pl.ds(step(b), 64) if isinstance(c, int) else pl.ds(pl.multiple_of(step(b), 64), 64),
                )
            for i, at in enumerate(spots(c)):
                out.send(2 * c + i, at)
            if do_in:
                da_s[top, :] = da_s[top, :] + dot_nt(dh, fin[:, cols])

        def last(i, at, carry):
            xhat, inv = normalise(x_s[at, :])
            da = da_s[at, :]
            g_s[at, :] = g_s[at, :] + norm_back(da, xhat, inv, gain)
            return carry + fold(da * xhat)

        def small_chunks():
            buf[:, :, pl.ds(high, SMALL_ROWS), :] = jnp.zeros((2, 4, SMALL_ROWS, LANES), BF)
            rows_all = jnp.concatenate([small_ref[...]] + [ref[...] for ref in small_refs], axis=0)
            lines = SMALL_ROWS // 4
            rows_all = jnp.concatenate([rows_all, jnp.zeros((4 * lines - rows_all.shape[0], D), F32)], axis=0)
            for z in range(4):
                pair = []
                for q in range(2):
                    own = rows_all[:, z * 128 + q * 64 : z * 128 + q * 64 + 64]
                    pair.append(jnp.concatenate([own[i * lines : (i + 1) * lines] for i in range(4)], axis=1))
                out.put((z, pl.ds(high, lines), slice(None)), pair)

        low_spot = (every, pl.ds(high, SMALL_ROWS))

        def main(midway):
            for c in starts:
                c.wait()
            for c in chunk_in(1):
                c.start()
            midway()
            gain4_grad = blocks(rows, first, jnp.zeros((8, D), F32))
            each(FF // 512, rows, chunk)
            small_ref[...] = jnp.zeros(small_ref.shape, F32)
            if do_in:
                small_ref[0:1, :] = total(blocks(rows, last, jnp.zeros((8, D), F32)))
            small_ref[1:2, :] = total(gain4_grad)
            if others:
                small_chunks()
                out.send(8, low_spot)

        def finish():
            if others:
                out.wait(8, low_spot)
            for c in range(4):
                for i, at in enumerate(spots(c)):
                    out.wait(2 * c + i, at)

        return start, main, finish

    return run


def feed_spec(l, k, what, smalls, gains, xs, hs, fin, fout):
    vm = pltpu.VMEM
    do_out, do_in = what != "in", what != "out"
    lines = D * do_in + D * do_out + (SMALL_ROWS if smalls else 0)
    none = (8, D)
    return (
        functools.partial(feed_part, l, k, what),
        [(gains, VMEM), (xs, ANY), (hs, ANY), (fin, ANY), (fout, ANY)] + [(v, VMEM) for v in smalls],
        [
            (struct((4, lines, LANES), BF), ANY),
            (struct((4, lines, LANES), BF), ANY),
            (struct((8, D), F32), VMEM),
        ],
        [
            vm((CAP, D) if do_in else none, F32), vm((CAP, D) if k == 1 else none, F32), vm((CAP, FF), BF),
            vm((D, FF) if do_in else none, BF), vm((FF, D) if do_in else none, BF), vm((CAP, D), BF),
            vm((CAP, D) if do_in else none, BF), vm((CAP, D) if do_in else none, F32),
            vm((2, 4, lines, LANES), BF),
            pltpu.SemaphoreType.DMA((15,)), pltpu.SemaphoreType.DMA((18,)),
        ],
        (2 * do_out + 6 * do_in) * 640 * D * FF,
    )


def conv_part(l, core_ref, g_s, ins, outs, scratch):
    kb_ref, gains_ref, taps_ref, mean_ref, var_ref, scale_ref, shift_ref, xs_h, u_h, z_h, pin_h, pout_h = ins
    keep_h, send_h, small_ref = outs
    x_s, u_s, z_s, pin, pout, gl_s, a_s, e_s, de_s, gp, dzp, kp, du_s, buf, sem, osem = scratch
    gain = gains_ref[l, pl.ds(2, 1), :]
    rs = lax.rsqrt(var_ref[pl.ds(l, 1), :] + EPSILON)
    mean = mean_ref[pl.ds(l, 1), :]
    scale = scale_ref[pl.ds(l, 1), :]
    shift = shift_ref[pl.ds(l, 1), :]
    out = Out(core_ref[0], buf, keep_h, send_h, osem)
    every = pl.ds(0, 4)

    def run(rows):
        top = pl.ds(0, rows)
        copies = [
            None,
            pltpu.make_async_copy(pout_h.at[l], pout, sem.at[1]),
            pltpu.make_async_copy(z_h.at[l, top], z_s.at[top], sem.at[2]),
            pltpu.make_async_copy(u_h.at[l, top], u_s.at[top], sem.at[3]),
            pltpu.make_async_copy(xs_h.at[l, 2, top], x_s.at[top], sem.at[4]),
            pltpu.make_async_copy(pin_h.at[l], pin, sem.at[5]),
        ]
        low_spot = (every, pl.ds(256, 128))
        high_spot = (every, pl.ds(0, 256))

        def start():
            for c in copies[1:4]:
                c.start()

        def finish():
            out.wait(0, low_spot)
            out.wait(1, high_spot)

        return start, functools.partial(conv_work, rows, copies), finish

    def conv_work(rows, copies, midway):
        top = pl.ds(0, rows)
        low_spot = (every, pl.ds(256, 128))
        high_spot = (every, pl.ds(0, 256))
        for ref in (gp, dzp):
            ref[:, pl.ds(0, 8), :] = jnp.zeros((PAIRS, 8, 128), F32)
            ref[:, pl.ds(rows + 8, 8), :] = jnp.zeros((PAIRS, 8, 128), F32)
        kp[pl.ds(0, 8), :] = jnp.full((8, 128), -1.0, F32)
        kp[pl.ds(rows + 8, 8), :] = jnp.full((8, 128), -1.0, F32)

        def low(i, at, carry):
            gl_s[at, :] = g_s[at, :].astype(BF)
            kp[pl.ds(pl.multiple_of(i * BLK + 8, 8), BLK), :] = kb_ref[at, :]
            return carry

        blocks(rows, low)
        for c in copies[1:4]:
            c.wait()
        for c in copies[4:]:
            c.start()
        midway()
        de_s[top, :] = dot_nt(gl_s[top, :], pout[...])
        copies[4].wait()

        def first(i, at, carry):
            scale_grad, shift_grad = carry
            inner = pl.ds(pl.multiple_of(i * BLK + 8, 8), BLK)
            hat = (z_s[at, :] - mean) * rs
            b = hat * scale + shift
            sig = sigmoid(b)
            e_s[at, :] = (b * sig).astype(BF)
            db = de_s[at, :] * (sig * (1.0 + b * (1.0 - sig)))
            dz = (db * scale * rs).astype(BF).astype(F32)
            u1 = u_s[at, pl.ds(0, D)].astype(F32)
            u2 = u_s[at, pl.ds(D, D)].astype(F32)
            gated = (u1 * sigmoid(u2)).astype(BF).astype(F32)
            for p in range(PAIRS):
                dzp[p, inner, :] = dz[:, p * 128 : (p + 1) * 128]
                gp[p, inner, :] = gated[:, p * 128 : (p + 1) * 128]
            xhat, _ = normalise(x_s[at, :])
            a_s[at, :] = (xhat * gain).astype(BF)
            return (scale_grad + fold(db * hat), shift_grad + fold(db))

        zero = jnp.zeros((8, D), F32)
        scale_grad, shift_grad = blocks(rows, first, (zero, zero))
        small_ref[...] = jnp.zeros(small_ref.shape, F32)
        small_ref[1:2, :] = total(scale_grad)
        small_ref[2:3, :] = total(shift_grad)
        dwo = dot_tn(gl_s[top, :], e_s[top, :])
        transposed_out(out, dwo, lambda b: pl.ds(256 + b * 64, 64))
        out.send(0, low_spot)

        for p in range(PAIRS):
            lanes = slice(p * 128, (p + 1) * 128)

            def taps(t, at, carry, lanes=lanes, p=p):
                own = kb_ref[at, :]
                dz_own = dzp[p, pl.ds(pl.multiple_of(t * BLK + 8, 8), BLK), :]
                dg = jnp.zeros((BLK, 128), F32)
                sums = []
                for o in range(KERNEL):
                    near = pl.ds(t * BLK + 4 + o, BLK)
                    mask = kp[near, :] == own
                    sums.append(carry[o] + fold(jnp.where(mask, dz_own * gp[p, near, :], 0.0)))
                    w = taps_ref[l, KERNEL - 1 - o : KERNEL - o, lanes]
                    dg = dg + jnp.where(mask, w * dzp[p, near, :], 0.0)
                u1 = u_s[at, lanes].astype(F32)
                sig = sigmoid(u_s[at, D + p * 128 : D + (p + 1) * 128].astype(F32))
                du_s[at, lanes] = (dg * sig).astype(BF)
                du_s[at, D + p * 128 : D + (p + 1) * 128] = (dg * u1 * sig * (1.0 - sig)).astype(BF)
                return tuple(sums)

            sums = blocks(rows, taps, tuple(jnp.zeros((8, 128), F32) for _ in range(KERNEL)))
            for o in range(KERNEL):
                small_ref[8 + o : 9 + o, lanes] = total(sums[o])

        for half in range(2):
            dwi = dot_tn(a_s[top, :], du_s[top, half * 512 : (half + 1) * 512])
            for q in range(2):
                pair = [
                    jnp.concatenate([dwi[: D // 2, at : at + 128], dwi[D // 2 :, at : at + 128]], axis=1)
                    for at in (q * 256, q * 256 + 128)
                ]
                out.put((2 * half + q, pl.ds(0, 256), slice(None)), pair)
        out.send(1, high_spot)
        copies[5].wait()
        de_s[top, :] = dot_nt(du_s[top, :], pin[...])

        def last(i, at, carry):
            xhat, inv = normalise(x_s[at, :])
            da = de_s[at, :]
            g_s[at, :] = g_s[at, :] + norm_back(da, xhat, inv, gain)
            return carry + fold(da * xhat)

        small_ref[0:1, :] = total(blocks(rows, last, zero))

    return run


def conv_spec(l, kb, small, xs, u, z, pin, pout):
    vm = pltpu.VMEM
    return (
        functools.partial(conv_part, l),
        [(kb, VMEM)] + [(v, VMEM) for v in small] + [(v, ANY) for v in (xs, u, z, pin, pout)],
        [
            (struct((4, 384, LANES), BF), ANY),
            (struct((4, 384, LANES), BF), ANY),
            (struct((24, D), F32), VMEM),
        ],
        [
            vm((CAP, D), F32), vm((CAP, 2 * D), BF), vm((CAP, D), F32), vm((D, 2 * D), BF),
            vm((D, D), BF), vm((CAP, D), BF), vm((CAP, D), BF), vm((CAP, D), BF), vm((CAP, D), F32),
            vm((PAIRS, CAP + 16, 128), F32), vm((PAIRS, CAP + 16, 128), F32), vm((CAP + 16, 128), F32),
            vm((CAP, 2 * D), BF), vm((2, 4, 384, LANES), BF),
            pltpu.SemaphoreType.DMA((6,)), pltpu.SemaphoreType.DMA((4,)),
        ],
        12 * 640 * D * D,
    )


def attend_part(l, core_ref, g_s, ins, outs, scratch):
    cos_ref, sin_ref, gains_ref, xs_h, q_h, kv_h, at_h, o_h, ain_h, aout_h = ins
    keep_h, send_h, small_ref = outs
    x_s, q_s, kv_s, at_s, o_s, ain, aout, gl_s, a_s, do_s, dq_s, dkv_s, dp_s, da_s, buf, sem, osem = scratch
    out = Out(core_ref[0], buf, keep_h, send_h, osem)
    every = pl.ds(0, 4)
    gain = gains_ref[l, pl.ds(1, 1), :]

    def run(rows):
        tiles = rows // BLK
        top = pl.ds(0, rows)
        wide = pl.ds(0, rows + 2 * BLK)
        copies = [
            pltpu.make_async_copy(aout_h.at[l], aout, sem.at[0]),
            pltpu.make_async_copy(o_h.at[l, top], o_s.at[top], sem.at[1]),
            pltpu.make_async_copy(q_h.at[l, top], q_s.at[top], sem.at[2]),
            pltpu.make_async_copy(kv_h.at[l, wide], kv_s.at[wide], sem.at[3]),
            pltpu.make_async_copy(xs_h.at[l, 1, top], x_s.at[top], sem.at[5]),
            pltpu.make_async_copy(ain_h.at[l], ain, sem.at[6]),
        ]
        copies = [None] + copies

        def weights_in(t):
            return pltpu.make_async_copy(at_h.at[l, t], at_s.at[t], sem.at[8 + t])

        low_spot = (every, pl.ds(384, 128))
        high_spot = (every, pl.ds(0, 384))

        def start():
            for c in copies[1:5]:
                c.start()
            weights_in(0).start()

        def finish():
            out.wait(0, low_spot)
            out.wait(1, high_spot)

        return start, functools.partial(attend_work, rows, copies, weights_in), finish

    def attend_work(rows, copies, weights_in, midway):
        tiles = rows // BLK
        top = pl.ds(0, rows)
        low_spot = (every, pl.ds(384, 128))
        high_spot = (every, pl.ds(0, 384))

        def low(i, at, carry):
            gl_s[at, :] = g_s[at, :].astype(BF)
            return carry

        blocks(rows, low)

        def clear(i, at, carry):
            dkv_s[at, :] = jnp.zeros((BLK, 2 * D), F32)
            return carry

        blocks(rows + 2 * BLK, clear)
        copies[1].wait()
        do_s[top, :] = dot_nt(gl_s[top, :], aout[...]).astype(BF)
        for c in copies[2:5]:
            c.wait()
        for c in copies[5:]:
            c.start()
        midway()

        def tile(t, at, carry):
            near = pl.ds(pl.multiple_of(t * BLK, BLK), 3 * BLK)
            weights_in(t).wait()

            @pl.when(t + 1 < tiles)
            def _():
                weights_in(t + 1).start()

            for p in range(PAIRS):
                lanes = slice(p * 128, (p + 1) * 128)
                vlanes = slice(D + p * 128, D + (p + 1) * 128)
                do = stacked(do_s[at, lanes])
                low = at_s[t, p]
                weights = low.astype(F32)
                da = dot_nt(kv_s[near, vlanes], do)
                delta = jnp.sum(weights * da, axis=0, keepdims=True)
                ds = (weights * (da - delta)).astype(BF)
                dq_s[at, lanes] = unstacked(dot_tn(ds, kv_s[near, lanes])) * HD**-0.5
                dkv_s[near, lanes] = dkv_s[near, lanes] + dot_nn(ds, stacked(q_s[at, lanes]))
                dkv_s[near, vlanes] = dkv_s[near, vlanes] + dot_nn(low, do)
            return carry

        blocks(rows, tile)
        copies[5].wait()

        def turn(i, at, carry):
            inner = pl.ds(pl.multiple_of(i * BLK + BLK, BLK), BLK)
            cos, sin = cos_ref[at, :], sin_ref[at, :]
            for p in range(PAIRS):
                lanes = slice(p * 128, (p + 1) * 128)
                dq = dq_s[at, lanes]
                dk = dkv_s[inner, lanes]
                dp_s[at, lanes] = (dq * cos - swap_halves(dq) * sin).astype(BF)
                dp_s[at, D + p * 128 : D + (p + 1) * 128] = (dk * cos - swap_halves(dk) * sin).astype(BF)
                dp_s[at, 2 * D + p * 128 : 2 * D + (p + 1) * 128] = dkv_s[
                    inner, D + p * 128 : D + (p + 1) * 128
                ].astype(BF)
            xhat, _ = normalise(x_s[at, :])
            a_s[at, :] = (xhat * gain).astype(BF)
            return carry

        blocks(rows, turn)

        dwo = dot_tn(gl_s[top, :], o_s[top, :])
        transposed_out(out, dwo, lambda b: pl.ds(384 + b * 64, 64))
        out.send(0, low_spot)
        for half in range(2):
            dwi = dot_tn(dp_s[top, half * 768 : (half + 1) * 768], a_s[top, :])
            for q in range(2):
                for b in range(2):
                    pair = [
                        dwi[q * 384 + r * 192 : q * 384 + (r + 1) * 192, b * LANES : (b + 1) * LANES] for r in range(2)
                    ]
                    out.put((2 * half + q, pl.ds(b * 192, 192), slice(None)), pair)
        out.send(1, high_spot)
        copies[6].wait()
        da_s[top, :] = dot_nt(dp_s[top, :], ain[...])

        def last(i, at, carry):
            xhat, inv = normalise(x_s[at, :])
            da = da_s[at, :]
            g_s[at, :] = g_s[at, :] + norm_back(da, xhat, inv, gain)
            return carry + fold(da * xhat)

        small_ref[0:1, :] = total(blocks(rows, last, jnp.zeros((8, D), F32)))

    return run


def attend_spec(l, cos, sin, gains, xs, q, kv, at, o, ain, aout):
    vm = pltpu.VMEM
    return (
        functools.partial(attend_part, l),
        [(v, VMEM) for v in (cos, sin, gains)] + [(v, ANY) for v in (xs, q, kv, at, o, ain, aout)],
        [
            (struct((4, 512, LANES), BF), ANY),
            (struct((4, 512, LANES), BF), ANY),
            (struct((8, D), F32), VMEM),
        ],
        [
            vm((CAP, D), F32), vm((CAP, D), BF), vm((CAP + 2 * BLK, 2 * D), BF),
            vm((CAP // BLK, PAIRS, 3 * BLK, 2 * BLK), BF), vm((CAP, D), BF), vm((D, 3 * D), BF), vm((D, D), BF),
            vm((CAP, D), BF), vm((CAP, D), BF), vm((CAP, D), BF), vm((CAP, D), F32),
            vm((CAP + 2 * BLK, 2 * D), F32), vm((CAP, 3 * D), BF), vm((CAP, D), F32),
            vm((2, 4, 512, LANES), BF),
            pltpu.SemaphoreType.DMA((8 + CAP // BLK,)), pltpu.SemaphoreType.DMA((4,)),
        ],
        16 * 640 * D * D,
    )


def run_parts(name, n, core, g, specs, deps):
    in_counts = [len(spec[1]) for spec in specs]
    out_counts = [len(spec[2]) for spec in specs]
    scratch_counts = [len(spec[3]) for spec in specs]

    def taken(refs, counts):
        pieces, off = [], 0
        for count in counts:
            pieces.append(refs[off : off + count])
            off += count
        return pieces

    def body(n_ref, core_ref, g_h, *refs):
        ins, refs = refs[: sum(in_counts)], refs[sum(in_counts) :]
        out_h, *outs = refs[: 1 + sum(out_counts)]
        g_s, g_sem, *scratch = refs[1 + sum(out_counts) :]
        parts = [
            spec[0](core_ref, g_s, *piece)
            for spec, *piece in zip(
                specs, taken(ins, in_counts), taken(outs, out_counts), taken(scratch, scratch_counts)
            )
        ]

        def run(rows):
            top = pl.ds(0, rows)
            steps = [part(rows) for part in parts]
            g_in = pltpu.make_async_copy(g_h.at[top], g_s.at[top], g_sem)
            g_in.start()
            steps[0][0]()
            g_in.wait()
            for i, (_, main, _) in enumerate(steps):
                main(steps[i + 1][0] if i + 1 < len(steps) else lambda: None)
            g_out = pltpu.make_async_copy(g_s.at[top], out_h.at[top], g_sem)
            g_out.start()
            for _, _, finish in steps:
                finish()
            g_out.wait()

        by_rows(n_ref, run)

    outs = [(struct((CAP, D), F32), ANY)] + [out for spec in specs for out in spec[2]]
    g, *rest = call(
        body,
        [SMEM, SMEM, ANY] + [where for spec in specs for _, where in spec[1]],
        outs,
        [pltpu.VMEM((CAP, D), F32), pltpu.SemaphoreType.DMA] + [v for spec in specs for v in spec[3]],
        (n, core, g, *(v for spec in specs for v, _ in spec[1])),
        flops=sum(spec[4] for spec in specs),
        moved=16 * 2**20,
        name=name,
        deps=deps,
    )
    return g, taken(rest, out_counts)


def add(*terms):
    acc = terms[0].astype(F32)
    for term in terms[1:]:
        acc = acc + term.astype(F32)
    return acc.astype(BF)


def spot_of(place_ref):
    x, y, core = place_ref[0], place_ref[1], place_ref[3]
    even = core == 0
    return jnp.where(even, x, y), jnp.where(even, y, x), 1 + core, 2 - core


def split_first_body(sizes, place_ref, *refs):
    count = len(sizes)
    keeps, gots = refs[:count], refs[count : 2 * count]
    kept, sent = refs[2 * count :]
    first, _, by_first, by_second = spot_of(place_ref)
    off = 0
    for keep, got, n in zip(keeps, gots, sizes):
        at = pl.ds(off, n)

        def one(z, carry, keep=keep, got=got, at=at):
            for j in range(2):
                own = first * by_first + j * by_second
                other = (1 - first) * by_first + j * by_second
                kept[z, j, at] = add(keep[z, own], got[z, own])
                sent[z, j, at] = add(keep[z, other], got[z, other])
            return carry

        lax.fori_loop(0, 4, one, jnp.int32(0))
        off += n


def split_second_body(place_ref, keep, got, kept, sent):
    _, second, _, _ = spot_of(place_ref)

    def one(z, carry):
        kept[z] = add(keep[z, second], got[z, second])
        sent[z] = add(keep[z, 1 - second], got[z, 1 - second])
        return carry

    lax.fori_loop(0, 4, one, jnp.int32(0))


def split_z_body(plan, place_ref, *refs):
    ins, outs = refs[:-4], refs[-4:]
    z = place_ref[2]
    for k, ref in enumerate(outs):
        at = lax.rem(z + k, 4)
        off = used = 0
        for count, n in plan:
            terms = [r[at] for r in ins[used : used + count]]
            ref[pl.ds(off, n), :] = add(*terms) if count > 1 else terms[0]
            used += count
            off += n


def row_pairs(bit):
    return [(i, i ^ bit) for i in range(4)]


def along(axis):
    return [(r * 8 + t, (r ^ (1 << ((t + axis) % 2))) * 8 + t) for r in range(4) for t in range(8)]


def sum_cores_body(sizes, *refs):
    count = len(sizes)
    keeps, gots, out = refs[:count], refs[count : 2 * count], refs[2 * count]
    off = 0
    for keep, got, n in zip(keeps, gots, sizes):
        at = pl.ds(off, n)

        def one(z, carry, keep=keep, got=got, at=at):
            for j in range(4):
                out[j, z, at] = add(keep[z, j], got[z, j])
            return carry

        lax.fori_loop(0, 4, one, jnp.int32(0))
        off += n


class Group:
    def __init__(self, spot, members):
        self.spot = spot
        self.keeps = [keep for _, keep, _ in members]
        self.sizes = [keep.shape[1] // 4 for keep in self.keeps]
        self.names = [name for name, _, _ in members]
        self.n = sum(self.sizes)
        self.bytes = 16 * self.n * LANES * 2
        self.gots = [got for _, _, got in members]

    def cores(self):
        shaped = lambda v: v.reshape(4, 4, v.shape[1] // 4, LANES)
        return (*map(shaped, self.keeps), *map(shaped, self.gots))

    def offload(self, deps):
        both = call(
            functools.partial(sum_cores_body, self.sizes),
            [VMEM] * (2 * len(self.sizes)),
            [(struct((4, 4, self.n, LANES), BF), VMEM)],
            [],
            self.cores(),
            moved=3 * self.bytes,
            name="sum_cores",
            vmem=VMEM_SMALL,
            deps=deps,
        )[0]
        part = lax.psum_scatter(both, "rows", scatter_dimension=0, tiled=True)
        self.terms = [part.reshape(4, self.n, LANES)]
        return [both]

    def first(self, deps, work=0):
        self.kept, sent = call(
            functools.partial(split_first_body, self.sizes),
            [SMEM] + [VMEM] * (2 * len(self.sizes)),
            [(struct((4, 2, self.n, LANES), BF), VMEM)] * 2,
            [],
            (self.spot, *self.cores()),
            moved=3 * self.bytes,
            name="split_first",
            vmem=VMEM_SMALL,
            flops=work,
            deps=deps,
        )
        self.got = lax.ppermute(sent, ("rows", "tm"), along(0))
        return [self.kept]

    def second(self, deps, work=0):
        self.kept, sent = call(
            split_second_body,
            [SMEM] + [VMEM] * 2,
            [(struct((4, self.n, LANES), BF), VMEM)] * 2,
            [],
            (self.spot, self.kept, self.got),
            moved=3 * self.bytes // 2,
            name="split_second",
            vmem=VMEM_SMALL,
            flops=work,
            deps=deps,
        )
        self.terms = [self.kept, lax.ppermute(sent, ("rows", "tm"), along(1))]
        return [self.kept]


def merge_body(*refs):
    *ins, out = refs
    off = 0
    for ref in ins:
        n = ref.shape[1]
        out[:, pl.ds(off, n), :] = ref[...]
        off += n


def offloaded_rest(groups, deps):
    n = sum(group.n for group in groups)
    part = call(
        merge_body,
        [VMEM] * len(groups),
        [(struct((4, n, LANES), BF), VMEM)],
        [],
        [group.terms[0] for group in groups],
        moved=16 * n * LANES,
        name="merge",
        vmem=VMEM_SMALL,
        deps=deps,
    )[0]
    mine = lax.psum_scatter(
        part, "tm", scatter_dimension=0, tiled=True, axis_index_groups=[[0, 2, 4, 6], [1, 3, 5, 7]]
    )
    mine = mine.reshape(part.shape[1:])
    return mine, lax.all_gather(mine, "rows", axis=0, tiled=True)


def along_z(spot, groups, deps, work=0):
    ins = [term for group in groups for term in group.terms]
    n = sum(group.n for group in groups)
    own, *others = call(
        functools.partial(split_z_body, [(len(group.terms), group.n) for group in groups]),
        [SMEM] + [VMEM] * len(ins),
        [(struct((n, LANES), BF), VMEM)] * 4,
        [],
        (spot, *ins),
        moved=16 * n * LANES * 2,
        name="split_z",
        vmem=VMEM_SMALL,
        flops=work,
        deps=deps,
    )
    return [own] + [
        lax.ppermute(v, "tm", [(i, (i + 2 * k) % 8) for i in range(8)]) for k, v in zip((1, 2, 3), others)
    ]


def join_body(plan, *refs):
    *ins, out = refs
    off = at = 0
    for count, n in plan:
        out[pl.ds(at, n), :] = add(*(ref[...] for ref in ins[off : off + count])) if count > 1 else ins[off][...]
        off += count
        at += n


def gathered(lists, deps):
    ins = [term for terms in lists for term in terms]
    plan = [(len(terms), terms[0].shape[0]) for terms in lists]
    n = sum(rows for _, rows in plan)
    mine = call(
        functools.partial(join_body, plan),
        [VMEM] * len(ins),
        [(struct((n, LANES), BF), VMEM)],
        [],
        ins,
        moved=6 * n * LANES,
        name="join",
        vmem=VMEM_SMALL,
        deps=deps,
    )[0]
    return [mine] + [lax.ppermute(mine, "rows", row_pairs(bit)) for bit in (1, 2, 3)]


def finish_body(members, by_bit, me_ref, *refs):
    count = 4 if by_bit else 1
    chunks = refs[:count]
    fin_h, fout_h, ain_h, aout_h, pin_h, pout_h, small_h = refs[-13:-6]
    whole, fout, ain, pin, narrow, sem = refs[-6:]
    me = me_ref[0]
    rows = sum(n for _, _, n in members)
    off = 0
    waits = []
    for i, (l, name, n) in enumerate(members):
        for j in range(4):
            if by_bit:
                owner = pl.multiple_of(jnp.bitwise_xor(me, j) * n, n)
                whole[i, pl.ds(owner, n), :] = chunks[j][pl.ds(off, n), :].astype(F32)
            else:
                whole[i, pl.ds(j * n, n), :] = chunks[0][pl.ds(j * rows + off, n), :].astype(F32)
        off += n
        if name in ("f0", "f1", "f0in", "f0out"):
            k = int(name == "f1")
            jobs = []
            if name != "f0out":
                jobs.append((whole.at[i, pl.ds(0, D)], fin_h.at[l, k]))
            if name != "f0in":
                base = 0 if name == "f0out" else D
                for b in range(FF // LANES):
                    fout[i, :, pl.ds(b * LANES, LANES)] = whole[i, pl.ds(base + b * 64, 64), :]
                jobs.append((fout.at[i], fout_h.at[l, k]))
            else:
                jobs.append((whole.at[i, pl.ds(D, SMALL_ROWS // 4)], small_h))
        elif name == "c":
            pin[i, pl.ds(0, 256), :] = whole[i, pl.ds(0, 256), 0:128]
            pin[i, pl.ds(256, 256), :] = whole[i, pl.ds(0, 256), 128:256]
            for b in range(2):
                narrow[i, :, pl.ds(b * LANES, LANES)] = whole[i, pl.ds(256 + b * 64, 64), :]
            jobs = [(pin.at[i], pin_h.at[l]), (narrow.at[i], pout_h.at[l])]
        else:
            for b in range(2):
                ain[i, :, pl.ds(b * LANES, LANES)] = whole[i, pl.ds(b * 192, 192), :]
                narrow[i, :, pl.ds(b * LANES, LANES)] = whole[i, pl.ds(384 + b * 64, 64), :]
            jobs = [(ain.at[i], ain_h.at[l]), (narrow.at[i], aout_h.at[l])]
        for j, (src, dst) in enumerate(jobs):
            c = pltpu.make_async_copy(src, dst, sem.at[3 * i + j])
            c.start()
            waits.append(c)
    for c in waits:
        c.wait()


def finish(layers, me, groups, chunks, before, deps=()):
    members = [(*name, size) for group in groups for name, size in zip(group.names, group.sizes)]
    count = len(members)
    shapes = [
        (layers, 2, D, FF // 8), (layers, 2, D // 8, FF), (layers, 3 * D // 8, D), (layers, D // 8, D),
        (layers, D, 2 * D // 8), (layers, D // 8, D), (SMALL_ROWS // 4, LANES),
    ]
    vm = pltpu.VMEM

    def body(*refs):
        finish_body(members, len(chunks) == 4, *refs)

    return pl.pallas_call(
        body,
        out_shape=[struct(shape, F32) for shape in shapes],
        in_specs=[SMEM] + [VMEM] * len(chunks) + [ANY] * (len(before) + len(deps)),
        out_specs=[ANY] * 7,
        scratch_shapes=[
            vm((count, 1024 + SMALL_ROWS, LANES), F32), vm((count, 64, FF), F32), vm((count, 192, D), F32),
            vm((count, D, 128), F32), vm((count, 64, D), F32), pltpu.SemaphoreType.DMA((3 * count,)),
        ],
        input_output_aliases={1 + len(chunks) + i: i for i in range(len(before))},
        compiler_params=pltpu.CompilerParams(vmem_limit_bytes=VMEM_LIMIT),
        name="finish",
    )(me, *chunks, *before, *deps)


def per_device(
    frames, segment_ids, norm_gains, feed_in, feed_out, attend_in, attend_out, point_in, depthwise, stat_mean,
    stat_var, batch_scale, batch_shift, point_out, cotangent,
):
    batches, row_count, frame_count, model_dim = frames.shape
    layers = norm_gains.shape[0]
    tm_size = lax.axis_size("tm")
    rows_size = lax.axis_size("rows")
    tm = lax.axis_index("tm")
    row = lax.axis_index("rows")
    fast = tm_size == 8 and rows_size == 4
    half = batches // 2

    ids = segment_ids[:, 0] + 1
    id_rows = jnp.broadcast_to(ids.reshape(1, -1).astype(BF), (16, batches * frame_count))
    parts_of = lambda v, odd: v.reshape(half, 2, frame_count, model_dim)[:, odd].reshape(-1, model_dim)
    message = lambda odd: jnp.concatenate([parts_of(frames, odd), parts_of(cotangent, odd), id_rows], axis=0)
    above = shifted(message(0), "tm", -1)
    below = shifted(message(1), "tm", 1)
    flat = lambda v: v.reshape(batches * frame_count, model_dim)
    x0, g, chooser, cos, sin, kb, kr, n = pack(ids.astype(F32), flat(frames), flat(cotangent), below, above)
    small = (norm_gains, depthwise, stat_mean, stat_var, batch_scale, batch_shift)
    mats = (feed_in, feed_out, attend_in, attend_out, point_in, point_out)
    act, xs, hs, q, kv, at, o, u, z = forward(n, x0, cos, sin, kb, kr, small, mats)

    def unpacked(packed):
        spread = lax.dot_general(
            chooser, packed, (((0,), (0,)), ((), ())), preferred_element_type=F32
        ).astype(BF).reshape(half, 2, 2, frame_count, model_dim)
        from_below = shifted(spread[:, 0, 1], "tm", 1)
        from_above = shifted(spread[:, 1, 0], "tm", -1)
        even = spread[:, 0, 0] + from_below
        odd = spread[:, 1, 1] + from_above
        return jnp.stack([even, odd], axis=1).reshape(batches, 1, frame_count, model_dim)

    activations = unpacked(act)

    if fast:
        spot = jnp.stack([row % 2, row // 2, tm // 2, tm % 2]).astype(jnp.int32)
        core = (tm % 2).astype(jnp.int32).reshape(1)
    else:
        spot = None
        core = jnp.zeros((1,), jnp.int32)

    members = {}
    smalls = {}
    parts = {
        "f1": lambda l: feed_spec(l, 1, "all", (), norm_gains, xs, hs, feed_in, feed_out),
        "c": lambda l: conv_spec(l, kb, small, xs, u, z, point_in, point_out),
        "a": lambda l: attend_spec(l, cos, sin, norm_gains, xs, q, kv, at, o, attend_in, attend_out),
        "f0": lambda l: feed_spec(l, 0, "all", (), norm_gains, xs, hs, feed_in, feed_out),
        "f0out": lambda l: feed_spec(l, 0, "out", (), norm_gains, xs, hs, feed_in, feed_out),
        "f0in": lambda l, rest: feed_spec(l, 0, "in", rest, norm_gains, xs, hs, feed_in, feed_out),
    }
    order = [(l, name) for l in range(layers) for name in ("f0", "a", "c", "f1")]

    def back(l, *names, deps=(), **more):
        nonlocal g
        specs = [parts[name](l, **more) for name in names]
        g, outs = run_parts(f"back_{l}_{'_'.join(names)}", n, core, g, specs, deps)
        for name, (kept, sent, small_grads) in zip(names, outs):
            smalls[l, name] = small_grads
            members[l, name] = ((l, name), kept, sent)

    crossed = {}

    def begin(l, name):
        crossed[l, name] = lax.ppermute(members[l, name][2], "tm", [(i, i ^ 1) for i in range(8)])

    def group(*names):
        for name in names:
            if name not in crossed:
                begin(*name)
        return Group(spot, [(name, members[name][1], crossed[name]) for name in names])

    if fast:
        me = (2 * spot[1] + spot[0]).reshape(1)
        back(1, "f1", "c")
        one = group((1, "f1"), (1, "c"))
        made = one.offload([])
        back(1, "a", "f0", deps=made)
        two = group((1, "a"), (1, "f0"))
        made = two.offload([])
        back(0, "f1", deps=made + one.terms)
        begin(0, "f1")
        back(0, "c")
        begin(0, "c")
        three = group((0, "f1"))
        made = three.first([g])
        mine_early, all_early = offloaded_rest([one, two], made)
        back(0, "a", "f0out", deps=made + two.terms)
        four = group((0, "c"), (0, "a"), (0, "f0out"))
        made = three.second([g])
        made += four.first(made)
        back(0, "f0in", deps=made + [mine_early], rest=[smalls[name] for name in order[1:]])
        five = group((0, "f0in"))
        z_three = along_z(spot, [three], [g], TAIL_WORK)
        made = five.first(z_three[:1])
        made = four.second(made)
        z_four = along_z(spot, [four], made)
        made = five.second(z_four[:1])
        outs = finish(layers, me, [one, two], [all_early], [], made)
        chunks_mid = gathered([z_three, z_four], outs[:1])
        z_five = along_z(spot, [five], chunks_mid[:1])
        outs = finish(layers, me, [three, four], chunks_mid, outs)
        chunks_late = gathered([z_five], outs[:1])
        *mats_out, small_out = finish(layers, me, [five], chunks_late, outs)
        mats_out = [
            v.swapaxes(-1, -2) if turned else v for v, turned in zip(mats_out, (False, True, True, True, False, True))
        ]
        lines = small_out.reshape(-1, 4, 64).swapaxes(0, 1).reshape(-1, 64)
        starts = {name: 0 for name in order}
        at_row = 0
        smalls[0, "f0"] = smalls[0, "f0in"]
        for name in order:
            starts[name] = at_row
            at_row += smalls[name].shape[0]
        pieces = lambda name, first, count: [
            lines[starts[l, name] + first : starts[l, name] + first + count] for l in range(layers)
        ]
    else:
        for l in reversed(range(layers)):
            back(l, "f1", "c")
            back(l, "a", "f0")
        pieces = None
    filled = lax.broadcasted_iota(jnp.int32, g.shape, 0) < n[0]
    frames_grad = unpacked(jnp.where(filled, g, 0.0).astype(BF))

    if not fast:
        mats_out, lines_of = general_sums(layers, members, smalls, order)
        pieces = lambda name, first, count: [lines_of[l, name][first : first + count] for l in range(layers)]
    gains_out = jnp.stack(
        [
            jnp.concatenate(rows, axis=0)
            for rows in zip(
                pieces("f0", 0, 1), pieces("a", 0, 1), pieces("c", 0, 1), pieces("f1", 0, 1), pieces("f1", 1, 1)
            )
        ]
    )
    fin, fout, ain, aout, pin, pout = mats_out
    return (
        activations,
        frames_grad,
        gains_out,
        fin,
        fout,
        ain,
        aout,
        pin,
        jnp.stack(pieces("c", 8, KERNEL)),
        jnp.concatenate(pieces("c", 1, 1), axis=0),
        jnp.concatenate(pieces("c", 2, 1), axis=0),
        pout,
    )


def general_sums(layers, members, smalls, order):
    def natural(l, name):
        _, even, odd = members[l, name]
        return jnp.stack([even, odd], axis=1).astype(F32).reshape(8, -1, LANES)

    def wide(v, count):
        r = v.shape[1] // count
        return jnp.swapaxes(v.reshape(8, count, r, LANES), 1, 2).reshape(8 * r, count * LANES)

    def over_all(v):
        v = lax.psum_scatter(v, "tm", scatter_dimension=v.ndim - 1, tiled=True)
        return lax.psum(v, "rows")

    fin, fout, ain, aout, pin, pout = [], [], [], [], [], []
    for l in range(layers):
        f = [natural(l, "f0"), natural(l, "f1")]
        fin.append(jnp.stack([jnp.moveaxis(v[:, :D], 0, 1).reshape(D, FF) for v in f]))
        fout.append(jnp.stack([wide(v[:, D:], FF // LANES).T for v in f]))
        v = natural(l, "a")
        ain.append(wide(v[:, :384], 2).T)
        aout.append(wide(v[:, 384:], 2).T)
        v = natural(l, "c")
        top = jnp.concatenate([v[:, :256, :128], v[:, :256, 128:]], axis=1)
        pin.append(jnp.moveaxis(top, 0, 1).reshape(D, 2 * D))
        pout.append(wide(v[:, 256:], 2).T)
    mats_out = [over_all(jnp.stack(v)) for v in (fin, fout, ain, aout, pin, pout)]
    small_all = over_all(jnp.concatenate([smalls[name] for name in order], axis=0))
    lines_of = {}
    at = 0
    for name in order:
        rows = smalls[name].shape[0]
        lines_of[name] = small_all[at : at + rows]
        at += rows
    return mats_out, lines_of


def solution(mesh):
    rep = P()
    in_specs = (
        P(None, "rows", "tm", None), P(None, "rows", "tm"), rep, rep, rep, rep, rep, rep, rep, rep, rep, rep, rep, rep,
        P(None, "rows", "tm", None),
    )
    out_specs = (
        P(None, "rows", "tm", None), P(None, "rows", "tm", None), P(None, None, "tm"), P(None, None, None, "tm"),
        P(None, None, None, "tm"), P(None, None, "tm"), P(None, None, "tm"), P(None, None, "tm"),
        P(None, None, "tm"), P(None, "tm"), P(None, "tm"), P(None, None, "tm"),
    )
    return jax.shard_map(per_device, mesh=mesh, in_specs=in_specs, out_specs=out_specs, check_vma=False)
```

profile of v0, /device:TPU:10, one launch (start us, length us, event | category | flops | bytes accessed | tf_op | source)
XLA Modules:
  0.0 367.0 jit_solution(5062061970345062409)
XLA Ops:
  10.7 1.9 collective-permute-start.1
  12.7 2.4 collective-permute-start
  16.3 3.2 collective-permute-done.1.refs_4_
  19.5 3.8 %collective-permute-done.refs_3_ = bf16[528,512]{1,0:T(8,128)(2,1)S(1)} collective-permute-done((bf16[528,512]{1,0:T(8,128)(2,1)S(1)}, bf16[528,512]{1,0:T(8,128)(2,1)S(1)}, u32[]{:S(2)}, u32[]{:S(2)}) %collective-permute-start) | collective-permute-done | bytes 540704 | tf_op jit(solution)/shard_map/ppermute | solution.py:37
  24.1 7.5 %pack.1 = (f32[1024,512]{1,0:T(8,128)}, f32[1024,512]{1,0:T(8,128)}, bf16[1024,1024]{1,0:T(8,128)(2,1)}, f32[1024,128]{1,0:T(8,128)}, f32[1024,128]{1,0:T(8,128)...) custom-call(f32[4,128]{1,0:T(4,128)} %get-tuple-element.251.refs_0_, bf16[512,512]{1,0:T(8,128)(2,1)} %bitcast.157, ...), custom_call_target="tpu_custom_call" | custom-call | flops 2147483648 | bytes 12582912 | tf_op jit(solution)/shard_map/pack/pallas_call | solution.py:50
  31.6 42.7 %forward.1 = (bf16[1024,512]{1,0:T(8,128)(2,1)}, f32[2,5,1024,512]{3,2,1,0:T(8,128)}, bf16[2,2,1024,2048]{3,2,1,0:T(8,128)(2,1)}, bf16[2,1024,512]{2,1,0:T(8,128...) custom-call(s32[1]{0:T(128)} %get-tuple-element.106.refs_0_, ...), custom_call_target="tpu_custom_call" | custom-call | flops 15360000000 | bytes 62914560 | tf_op jit(solution)/shard_map/forward/pallas_call | solution.py:50
  74.3 32.4 %back_1_f1_c.1 = (f32[1024,512]{1,0:T(8,128)}, bf16[4,1024,256]{2,1,0:T(8,128)(2,1)}, bf16[4,1024,256]{2,1,0:T(8,128)(2,1)}, f32[8,512]{1,0:T(8,128)}, bf16[4,38...) custom-call(s32[1]{0:T(128)} %get-tuple-element.106.refs_0_, s32[1]{0:T(128)} %bitcast.20.refs_1_, ...), custom_call_target="tpu_custom_call" | custom-call | flops 7381975040 | bytes 16777216 | tf_op jit(solution)/shard_map/back_1_f1_c/pallas_call | solution.py:50
  107.3 5.0 %collective-permute-done.5 = bf16[4,384,256]{2,1,0:T(8,128)(2,1)S(1)} collective-permute-done((bf16[4,384,256]{2,1,0:T(8,128)(2,1)}, bf16[4,384,256]{2,1,0:T(8,128)(2,1)S(1)}, u32[]{:S(2)}, u32[]{:S(2)}) %collective-permute-start.5) | collective-permute-done | bytes 786464 | tf_op jit(solution)/shard_map/ppermute | solution.py:1459
  115.0 2.3 sum_cores.2.refs_18_
  117.4 32.1 %back_1_a_f0.1 = (f32[1024,512]{1,0:T(8,128)}, bf16[4,512,256]{2,1,0:T(8,128)(2,1)}, bf16[4,512,256]{2,1,0:T(8,128)(2,1)}, f32[8,512]{1,0:T(8,128)}, bf16[4,1024...) custom-call(s32[1]{0:T(128)} %get-tuple-element.106.refs_0_, s32[1]{0:T(128)} %bitcast.20.refs_1_, ...), custom_call_target="tpu_custom_call" | custom-call | flops 8053063680 | bytes 16777216 | tf_op jit(solution)/shard_map/back_1_a_f0/pallas_call | solution.py:50
  150.0 5.4 %collective-permute-done.6 = bf16[4,512,256]{2,1,0:T(8,128)(2,1)S(1)} collective-permute-done((bf16[4,512,256]{2,1,0:T(8,128)(2,1)}, bf16[4,512,256]{2,1,0:T(8,128)(2,1)S(1)}, u32[]{:S(2)}, u32[]{:S(2)}) %collective-permute-start.6) | collective-permute-done | bytes 1048608 | tf_op jit(solution)/shard_map/ppermute | solution.py:1459
  158.2 2.4 sum_cores.3.refs_8_
  160.7 15.8 %back_0_f1.1 = (f32[1024,512]{1,0:T(8,128)}, bf16[4,1024,256]{2,1,0:T(8,128)(2,1)}, bf16[4,1024,256]{2,1,0:T(8,128)(2,1)}, f32[8,512]{1,0:T(8,128)}) custom-call(s32[1]{0:T(128)} %get-tuple-element.106.refs_0_, s32[1]{0:T(128)} %bitcast.20.refs_1_, f32[1024,512]{1,0:T(8,128)} %get-tuple-element.127.refs_2_, ...), custom_call_target="tpu_custom_call" | custom-call | flops 5368709120 | bytes 16777216 | tf_op jit(solution)/shard_map/back_0_f1/pallas_call | solution.py:50
  176.9 15.2 %back_0_c.1 = (f32[1024,512]{1,0:T(8,128)}, bf16[4,384,256]{2,1,0:T(8,128)(2,1)}, bf16[4,384,256]{2,1,0:T(8,128)(2,1)}, f32[24,512]{1,0:T(8,128)}) custom-call(s32[1]{0:T(128)} %get-tuple-element.106.refs_0_, s32[1]{0:T(128)} %bitcast.20.refs_1_, f32[1024,512]{1,0:T(8,128)} %get-tuple-element.132.refs_2_, ...), custom_call_target="tpu_custom_call" | custom-call | flops 2013265920 | bytes 16777216 | tf_op jit(solution)/shard_map/back_0_c/pallas_call | solution.py:50
  194.9 2.1 copy-done.13
  199.7 7.6 %reduce-scatter.12.cloned.1.call-done = bf16[1,4,384,256]{3,2,1,0:T(8,128)(2,1)} async-done(((bf16[4,4,384,256]{3,2,1,0:T(8,128)(2,1)}), bf16[1,4,384,256]{3,2,1,0:T(8,128)(2,1)}) %reduce-scatter.12.cloned.1.call-update) | async-done | bytes 786448
  210.5 25.1 %back_0_a_f0out.1 = (f32[1024,512]{1,0:T(8,128)}, bf16[4,512,256]{2,1,0:T(8,128)(2,1)}, bf16[4,512,256]{2,1,0:T(8,128)(2,1)}, f32[8,512]{1,0:T(8,128)}, bf16[4,5...) custom-call(s32[1]{0:T(128)} %get-tuple-element.106.refs_0_, s32[1]{0:T(128)} %bitcast.20.refs_1_, ...), custom_call_target="tpu_custom_call" | custom-call | flops 4026531840 | bytes 16777216 | tf_op jit(solution)/shard_map/back_0_a_f0out/pallas_call | solution.py:50
  244.3 3.6 split_first.4
  249.6 13.3 %back_0_f0in.1 = (f32[1024,512]{1,0:T(8,128)}, bf16[4,640,256]{2,1,0:T(8,128)(2,1)}, bf16[4,640,256]{2,1,0:T(8,128)(2,1)}, f32[8,512]{1,0:T(8,128)}) custom-call(s32[1]{0:T(128)} %get-tuple-element.106.refs_0_, s32[1]{0:T(128)} %bitcast.20.refs_1_, f32[1024,512]{1,0:T(8,128)} %get-tuple-element.137.refs_3_.refs_2_, ...), custom_call_target="tpu_custom_call" | custom-call | flops 4026531840 | bytes 16777216 | tf_op jit(solution)/shard_map/back_0_f0in/pallas_call | solution.py:50
  275.8 3.6 collective-permute-start.3
  280.1 8.8 %collective-permute-done.19.refs_2_ = bf16[4,352,256]{2,1,0:T(8,128)(2,1)S(1)} collective-permute-done((bf16[4,352,256]{2,1,0:T(8,128)(2,1)S(1)}, bf16[4,352,256]{2,1,0:T(8,128)(2,1)S(1)}, u32[]{:S(2)}, u32[]{:S(2)}) %collective-permute-start.19) | collective-permute-done | bytes 720928 | tf_op jit(solution)/shard_map/ppermute | solution.py:1237
  288.9 2.4 collective-permute-start.22
  296.9 3.6 collective-permute-done.22.refs_2_
  300.5 3.4 collective-permute-start.25
  304.6 7.5 %collective-permute-done.24.refs_5_ = bf16[352,256]{1,0:T(8,128)(2,1)S(1)} collective-permute-done((bf16[352,256]{1,0:T(8,128)(2,1)S(1)}, bf16[352,256]{1,0:T(8,128)(2,1)S(1)}, u32[]{:S(2)}, u32[]{:S(2)}) %collective-permute-start.24) | collective-permute-done | bytes 180256 | tf_op jit(solution)/shard_map/ppermute | solution.py:1286
  314.1 3.2 finish.3
  317.3 1.9 collective-permute-start.13
  319.3 3.6 collective-permute-start.14
  331.0 2.5 collective-permute-start.27
  333.5 2.4 collective-permute-done.32.refs_4_
  336.0 6.5 %collective-permute-done.31.refs_3_ = bf16[608,256]{1,0:T(8,128)(2,1)S(1)} collective-permute-done((bf16[608,256]{1,0:T(8,128)(2,1)S(1)}, bf16[608,256]{1,0:T(8,128)(2,1)S(1)}, u32[]{:S(2)}, u32[]{:S(2)}) %collective-permute-start.31) | collective-permute-done | bytes 311328 | tf_op jit(solution)/shard_map/ppermute | solution.py:1314
  343.3 2.9 finish.4
  (197 shorter events, 76.4 us)
Async XLA Ops:
  7.2 153.6 %reduce-scatter.10.cloned.1.call-start = ((), (), s32[]{:S(2)}) async-start(), calls=%async_computation.5 | async-start | bytes 3604480
  10.7 8.8 %collective-permute-start.1 = (bf16[528,512]{1,0:T(8,128)(2,1)S(1)}, bf16[528,512]{1,0:T(8,128)(2,1)S(1)}, u32[]{:S(2)}, u32[]{:S(2)}) collective-permute-start(bf16[528,512]{1,0:T(8,128)(2,1)S(1)} %get-tuple-element.248), channel_id=1, source_target_pairs={{1,0},{2,1},{3,2},{4,3},{5,4},{6,5},{7,6},{9,8},{10,9},{11,10},{12... | collective-permute-start | bytes 1622024 | tf_op jit(solution)/shard_map/ppermute | solution.py:37
  12.7 10.7 %collective-permute-start = (bf16[528,512]{1,0:T(8,128)(2,1)S(1)}, bf16[528,512]{1,0:T(8,128)(2,1)S(1)}, u32[]{:S(2)}, u32[]{:S(2)}) collective-permute-start(bf16[528,512]{1,0:T(8,128)(2,1)S(1)} %get-tuple-element.249), channel_id=1, source_target_pairs={{0,1},{1,2},{2,3},{3,4},{4,5},{5,6},{6,7},{8,9},{9,10},{10,11},{11... | collective-permute-start | bytes 1622024 | tf_op jit(solution)/shard_map/ppermute | solution.py:37
  117.3 90.0 %reduce-scatter.12.cloned.1.call-start = ((), (), s32[]{:S(2)}) async-start(), calls=%async_computation.6 | async-start | bytes 3932160
  160.7 88.9 %reduce-scatter.8.cloned.1.call-start = ((), (), s32[]{:S(2)}) async-start(), calls=%async_computation.3 | async-start | bytes 1884160 | tf_op jit(solution)/shard_map/reduce_scatter | solution.py:1263
  176.5 15.5 %collective-permute-start.8 = (bf16[4,1024,256]{2,1,0:T(8,128)(2,1)}, bf16[4,1024,256]{2,1,0:T(8,128)(2,1)S(1)}, u32[]{:S(2)}, u32[]{:S(2)}) collective-permute-start(bf16[4,1024,256]{2,1,0:T(8,128)(2,1)} %get-tuple-element.135), channel_id=1, source_target_pairs={{0,1},{1,0},{2,3},{3,2},{4,5},{5,4},{6,7},{7,6},{8,9},{9,8},{10,11... | collective-permute-start | bytes 6291464 | tf_op jit(solution)/shard_map/ppermute | solution.py:1459
  209.7 104.4 %all-gather.3.cloned.1.call-start = ((), (), s32[]{:S(2)}) async-start(), calls=%async_computation.4 | async-start | bytes 1884160 | tf_op jit(solution)/shard_map/all_gather | solution.py:1267
  209.8 26.5 %collective-permute-start.9 = (bf16[4,2,256,256]{3,2,1,0:T(8,128)(2,1)S(1)}, bf16[4,2,256,256]{3,2,1,0:T(8,128)(2,1)S(1)}, u32[]{:S(2)}, u32[]{:S(2)}) collective-permute-start(bf16[4,2,256,256]{3,2,1,0:T(8,128)(2,1)S(1)} %get-tuple-element.145), channel_id=1, source_target_pairs={{0,8},{1,17},{2,10},{3,19},{4,12},{5,21},{6,14},{7,23},{8,0},{9,25... | collective-permute-start | bytes 3145736 | tf_op jit(solution)/shard_map/ppermute | solution.py:1221
  235.6 7.5 %collective-permute-start.11 = (bf16[4,512,256]{2,1,0:T(8,128)(2,1)}, bf16[4,512,256]{2,1,0:T(8,128)(2,1)}, u32[]{:S(2)}, u32[]{:S(2)}) collective-permute-start(bf16[4,512,256]{2,1,0:T(8,128)(2,1)} %get-tuple-element.151), channel_id=1, source_target_pairs={{0,1},{1,0},{2,3},{3,2},{4,5},{5,4},{6,7},{7,6},{8,9},{9,8},{10,11... | collective-permute-start | bytes 3145736 | tf_op jit(solution)/shard_map/ppermute | solution.py:1459
  235.7 7.4 %collective-permute-start.12 = (bf16[4,512,256]{2,1,0:T(8,128)(2,1)}, bf16[4,512,256]{2,1,0:T(8,128)(2,1)}, u32[]{:S(2)}, u32[]{:S(2)}) collective-permute-start(bf16[4,512,256]{2,1,0:T(8,128)(2,1)} %get-tuple-element.152), channel_id=1, source_target_pairs={{0,1},{1,0},{2,3},{3,2},{4,5},{5,4},{6,7},{7,6},{8,9},{9,8},{10,11... | collective-permute-start | bytes 3145736 | tf_op jit(solution)/shard_map/ppermute | solution.py:1459
  236.2 6.9 %collective-permute-start.10 = (bf16[4,384,256]{2,1,0:T(8,128)(2,1)}, bf16[4,384,256]{2,1,0:T(8,128)(2,1)}, u32[]{:S(2)}, u32[]{:S(2)}) collective-permute-start(bf16[4,384,256]{2,1,0:T(8,128)(2,1)} %get-tuple-element.150), channel_id=1, source_target_pairs={{0,1},{1,0},{2,3},{3,2},{4,5},{5,4},{6,7},{7,6},{8,9},{9,8},{10,11... | collective-permute-start | bytes 2359304 | tf_op jit(solution)/shard_map/ppermute | solution.py:1459
  241.7 21.3 %collective-permute-start.16 = (bf16[4,256,256]{2,1,0:T(8,128)(2,1)}, bf16[4,256,256]{2,1,0:T(8,128)(2,1)}, u32[]{:S(2)}, u32[]{:S(2)}) collective-permute-start(bf16[4,256,256]{2,1,0:T(8,128)(2,1)} %get-tuple-element.157), channel_id=1, source_target_pairs={{0,16},{1,9},{2,18},{3,11},{4,20},{5,13},{6,22},{7,15},{8,24},{9,1... | collective-permute-start | bytes 1572872 | tf_op jit(solution)/shard_map/ppermute | solution.py:1237
  249.0 19.6 %collective-permute-start.18 = (bf16[4,2,352,256]{3,2,1,0:T(8,128)(2,1)}, bf16[4,2,352,256]{3,2,1,0:T(8,128)(2,1)S(1)}, u32[]{:S(2)}, u32[]{:S(2)}) collective-permute-start(bf16[4,2,352,256]{3,2,1,0:T(8,128)(2,1)} %get-tuple-element.161), channel_id=1, source_target_pairs={{0,8},{1,17},{2,10},{3,19},{4,12},{5,21},{6,14},{7,23},{8,0},{9,25... | collective-permute-start | bytes 4325384 | tf_op jit(solution)/shard_map/ppermute | solution.py:1221
  267.1 25.6 %collective-permute-start.17 = (bf16[4,2,160,256]{3,2,1,0:T(8,128)(2,1)S(1)}, bf16[4,2,160,256]{3,2,1,0:T(8,128)(2,1)S(1)}, u32[]{:S(2)}, u32[]{:S(2)}) collective-permute-start(bf16[4,2,160,256]{3,2,1,0:T(8,128)(2,1)S(1)} %get-tuple-element.160), channel_id=1, source_target_pairs={{0,8},{1,17},{2,10},{3,19},{4,12},{5,21},{6,14},{7,23},{8,0},{9,25... | collective-permute-start | bytes 1966088 | tf_op jit(solution)/shard_map/ppermute | solution.py:1221
  269.5 19.4 %collective-permute-start.19 = (bf16[4,352,256]{2,1,0:T(8,128)(2,1)S(1)}, bf16[4,352,256]{2,1,0:T(8,128)(2,1)S(1)}, u32[]{:S(2)}, u32[]{:S(2)}) collective-permute-start(bf16[4,352,256]{2,1,0:T(8,128)(2,1)S(1)} %get-tuple-element.163), channel_id=1, source_target_pairs={{0,16},{1,9},{2,18},{3,11},{4,20},{5,13},{6,22},{7,15},{8,24},{9,1... | collective-permute-start | bytes 2162696 | tf_op jit(solution)/shard_map/ppermute | solution.py:1237
  271.4 20.6 %collective-permute-start.21 = (bf16[256,256]{1,0:T(8,128)(2,1)S(1)}, bf16[256,256]{1,0:T(8,128)(2,1)S(1)}, u32[]{:S(2)}, u32[]{:S(2)}) collective-permute-start(bf16[256,256]{1,0:T(8,128)(2,1)S(1)} %get-tuple-element.167), channel_id=1, source_target_pairs={{0,2},{1,3},{2,4},{3,5},{4,6},{5,7},{6,0},{7,1},{8,10},{9,11},{10,... | collective-permute-start | bytes 393224 | tf_op jit(solution)/shard_map/ppermute | solution.py:1286
  273.8 50.9 %collective-permute-start.2 = (bf16[2,128,512]{2,1,0:T(8,128)(2,1)}, bf16[2,128,512]{2,1,0:T(8,128)(2,1)}, u32[]{:S(2)}, u32[]{:S(2)}) collective-permute-start(bf16[2,128,512]{2,1,0:T(8,128)(2,1)} %get-tuple-element.228), channel_id=1, source_target_pairs={{0,1},{1,2},{2,3},{3,4},{4,5},{5,6},{6,7},{8,9},{9,10},{10,11},{11... | collective-permute-start | bytes 786440 | tf_op jit(solution)/shard_map/ppermute | solution.py:37
  275.8 50.6 %collective-permute-start.3 = (bf16[2,128,512]{2,1,0:T(8,128)(2,1)}, bf16[2,128,512]{2,1,0:T(8,128)(2,1)}, u32[]{:S(2)}, u32[]{:S(2)}) collective-permute-start(bf16[2,128,512]{2,1,0:T(8,128)(2,1)} %get-tuple-element.229), channel_id=1, source_target_pairs={{1,0},{2,1},{3,2},{4,3},{5,4},{6,5},{7,6},{9,8},{10,9},{11,10},{12... | collective-permute-start | bytes 786440 | tf_op jit(solution)/shard_map/ppermute | solution.py:37
  288.9 11.6 %collective-permute-start.22 = (bf16[256,256]{1,0:T(8,128)(2,1)S(1)}, bf16[256,256]{1,0:T(8,128)(2,1)S(1)}, u32[]{:S(2)}, u32[]{:S(2)}) collective-permute-start(bf16[256,256]{1,0:T(8,128)(2,1)S(1)} %get-tuple-element.168), channel_id=1, source_target_pairs={{0,4},{1,5},{2,6},{3,7},{4,0},{5,1},{6,2},{7,3},{8,12},{9,13},{10,... | collective-permute-start | bytes 393224 | tf_op jit(solution)/shard_map/ppermute | solution.py:1286
  292.0 12.2 %collective-permute-start.23 = (bf16[256,256]{1,0:T(8,128)(2,1)S(1)}, bf16[256,256]{1,0:T(8,128)(2,1)S(1)}, u32[]{:S(2)}, u32[]{:S(2)}) collective-permute-start(bf16[256,256]{1,0:T(8,128)(2,1)S(1)} %get-tuple-element.169), channel_id=1, source_target_pairs={{0,6},{1,7},{2,0},{3,1},{4,2},{5,3},{6,4},{7,5},{8,14},{9,15},{10,... | collective-permute-start | bytes 393224 | tf_op jit(solution)/shard_map/ppermute | solution.py:1286
  292.6 19.5 %collective-permute-start.24 = (bf16[352,256]{1,0:T(8,128)(2,1)S(1)}, bf16[352,256]{1,0:T(8,128)(2,1)S(1)}, u32[]{:S(2)}, u32[]{:S(2)}) collective-permute-start(bf16[352,256]{1,0:T(8,128)(2,1)S(1)} %get-tuple-element.170), channel_id=1, source_target_pairs={{0,2},{1,3},{2,4},{3,5},{4,6},{5,7},{6,0},{7,1},{8,10},{9,11},{10,... | collective-permute-start | bytes 540680 | tf_op jit(solution)/shard_map/ppermute | solution.py:1286
  300.5 16.8 %collective-permute-start.25 = (bf16[352,256]{1,0:T(8,128)(2,1)S(1)}, bf16[352,256]{1,0:T(8,128)(2,1)S(1)}, u32[]{:S(2)}, u32[]{:S(2)}) collective-permute-start(bf16[352,256]{1,0:T(8,128)(2,1)S(1)} %get-tuple-element.171), channel_id=1, source_target_pairs={{0,4},{1,5},{2,6},{3,7},{4,0},{5,1},{6,2},{7,3},{8,12},{9,13},{10,... | collective-permute-start | bytes 540680 | tf_op jit(solution)/shard_map/ppermute | solution.py:1286
  304.2 15.0 %collective-permute-start.26 = (bf16[352,256]{1,0:T(8,128)(2,1)S(1)}, bf16[352,256]{1,0:T(8,128)(2,1)S(1)}, u32[]{:S(2)}, u32[]{:S(2)}) collective-permute-start(bf16[352,256]{1,0:T(8,128)(2,1)S(1)} %get-tuple-element.172), channel_id=1, source_target_pairs={{0,6},{1,7},{2,0},{3,1},{4,2},{5,3},{6,4},{7,5},{8,14},{9,15},{10,... | collective-permute-start | bytes 540680 | tf_op jit(solution)/shard_map/ppermute | solution.py:1286
  312.1 16.0 %collective-permute-start.20 = (bf16[4,160,256]{2,1,0:T(8,128)(2,1)S(1)}, bf16[4,160,256]{2,1,0:T(8,128)(2,1)S(1)}, u32[]{:S(2)}, u32[]{:S(2)}) collective-permute-start(bf16[4,160,256]{2,1,0:T(8,128)(2,1)S(1)} %get-tuple-element.166), channel_id=1, source_target_pairs={{0,16},{1,9},{2,18},{3,11},{4,20},{5,13},{6,22},{7,15},{8,24},{9,1... | collective-permute-start | bytes 983048 | tf_op jit(solution)/shard_map/ppermute | solution.py:1237
  317.3 13.6 %collective-permute-start.13 = (bf16[2,128,512]{2,1,0:T(8,128)(2,1)}, bf16[2,128,512]{2,1,0:T(8,128)(2,1)S(1)}, u32[]{:S(2)}, u32[]{:S(2)}) collective-permute-start(bf16[2,128,512]{2,1,0:T(8,128)(2,1)} %get-tuple-element.224), channel_id=1, source_target_pairs={{0,1},{1,2},{2,3},{3,4},{4,5},{5,6},{6,7},{8,9},{9,10},{10,11},{11... | collective-permute-start | bytes 786440 | tf_op jit(solution)/shard_map/ppermute | solution.py:37
  319.3 14.2 %collective-permute-start.14 = (bf16[2,128,512]{2,1,0:T(8,128)(2,1)}, bf16[2,128,512]{2,1,0:T(8,128)(2,1)S(1)}, u32[]{:S(2)}, u32[]{:S(2)}) collective-permute-start(bf16[2,128,512]{2,1,0:T(8,128)(2,1)} %get-tuple-element.225), channel_id=1, source_target_pairs={{1,0},{2,1},{3,2},{4,3},{5,4},{6,5},{7,6},{9,8},{10,9},{11,10},{12... | collective-permute-start | bytes 786440 | tf_op jit(solution)/shard_map/ppermute | solution.py:37
  324.7 11.2 %collective-permute-start.32 = (bf16[608,256]{1,0:T(8,128)(2,1)S(1)}, bf16[608,256]{1,0:T(8,128)(2,1)S(1)}, u32[]{:S(2)}, u32[]{:S(2)}) collective-permute-start(bf16[608,256]{1,0:T(8,128)(2,1)S(1)} %join.2.refs_3_.refs_1_), channel_id=1, source_target_pairs={{0,24},{8,16},{16,8},{24,0},{1,25},{9,17},{17,9},{25,1},{2,26},{10... | collective-permute-start | bytes 933896 | tf_op jit(solution)/shard_map/ppermute | solution.py:1314
  327.4 15.1 %collective-permute-start.31 = (bf16[608,256]{1,0:T(8,128)(2,1)S(1)}, bf16[608,256]{1,0:T(8,128)(2,1)S(1)}, u32[]{:S(2)}, u32[]{:S(2)}) collective-permute-start(bf16[608,256]{1,0:T(8,128)(2,1)S(1)} %join.2.refs_3_.refs_1_), channel_id=1, source_target_pairs={{0,16},{8,24},{16,0},{24,8},{1,17},{9,25},{17,1},{25,9},{2,18},{10... | collective-permute-start | bytes 933896 | tf_op jit(solution)/shard_map/ppermute | solution.py:1314
  328.1 14.4 %collective-permute-start.30 = (bf16[608,256]{1,0:T(8,128)(2,1)S(1)}, bf16[608,256]{1,0:T(8,128)(2,1)S(1)}, u32[]{:S(2)}, u32[]{:S(2)}) collective-permute-start(bf16[608,256]{1,0:T(8,128)(2,1)S(1)} %join.2.refs_3_.refs_1_), channel_id=1, source_target_pairs={{0,8},{8,0},{16,24},{24,16},{1,9},{9,1},{17,25},{25,17},{2,10},{10... | collective-permute-start | bytes 933896 | tf_op jit(solution)/shard_map/ppermute | solution.py:1314
  331.0 15.2 %collective-permute-start.27 = (bf16[160,256]{1,0:T(8,128)(2,1)S(1)}, bf16[160,256]{1,0:T(8,128)(2,1)S(1)}, u32[]{:S(2)}, u32[]{:S(2)}) collective-permute-start(bf16[160,256]{1,0:T(8,128)(2,1)S(1)} %get-tuple-element.175), channel_id=1, source_target_pairs={{0,2},{1,3},{2,4},{3,5},{4,6},{5,7},{6,0},{7,1},{8,10},{9,11},{10,... | collective-permute-start | bytes 245768 | tf_op jit(solution)/shard_map/ppermute | solution.py:1286
  333.5 12.7 %collective-permute-start.28 = (bf16[160,256]{1,0:T(8,128)(2,1)S(1)}, bf16[160,256]{1,0:T(8,128)(2,1)S(1)}, u32[]{:S(2)}, u32[]{:S(2)}) collective-permute-start(bf16[160,256]{1,0:T(8,128)(2,1)S(1)} %get-tuple-element.176), channel_id=1, source_target_pairs={{0,4},{1,5},{2,6},{3,7},{4,0},{5,1},{6,2},{7,3},{8,12},{9,13},{10,... | collective-permute-start | bytes 245768 | tf_op jit(solution)/shard_map/ppermute | solution.py:1286
  336.0 10.2 %collective-permute-start.29 = (bf16[160,256]{1,0:T(8,128)(2,1)S(1)}, bf16[160,256]{1,0:T(8,128)(2,1)S(1)}, u32[]{:S(2)}, u32[]{:S(2)}) collective-permute-start(bf16[160,256]{1,0:T(8,128)(2,1)S(1)} %get-tuple-element.177), channel_id=1, source_target_pairs={{0,6},{1,7},{2,0},{3,1},{4,2},{5,3},{6,4},{7,5},{8,14},{9,15},{10,... | collective-permute-start | bytes 245768 | tf_op jit(solution)/shard_map/ppermute | solution.py:1286
  (53 other events, 246.2 us)
Sparse Core Ops, SparseCore 0:
  117.4 42.8 reduce-scatter.9
  163.3 43.9 reduce-scatter.11
  209.8 32.4 reduce-scatter.7
  263.1 35.4 all-gather.2
where the time goes:
time: 373 us; the launch traced here: 367 us
  Pallas kernels  209 us (56%)
  waiting for transfers between devices  57.3 us (15%)
  starting transfers between devices  43.2 us (12%)
  local copies, waits for them, and re-layouts  36 us (10%)
  between operations  14.7 us (4%)
  other arithmetic  3.9 us (1%)
    pallas_call x22, Pallas kernels, call(): pl.pallas_call(inner, out_shape=[s for s, _ in outs], in_specs=list(ins)...  202 us
    unnamed x94, local copies, waits for them, and re-layouts  29.6 us
    ppermute x6, starting transfers between devices, shifted(): return lax.ppermute(array, axis, pairs)  15.4 us
    ppermute x9, starting transfers between devices, along_z(): lax.ppermute(v, 'tm', [(i, (i + 2 * k) % 8) for i in range(8)])  12.3 us
    ppermute x6, waiting for transfers between devices, gathered(): lax.ppermute(mine, 'rows', row_pairs(bit))  11.6 us
    ppermute x9, waiting for transfers between devices, along_z(): lax.ppermute(v, 'tm', [(i, (i + 2 * k) % 8) for i in range(8)])  11.5 us
    ppermute x9, waiting for transfers between devices, begin(): lax.ppermute(members[l, name][2], 'tm', [(i, i ^ 1) for i in range(8)])  10.7 us
    ppermute x3, waiting for transfers between devices, second(): self.terms = [self.kept, lax.ppermute(sent, ('rows', 'tm'), along(1))]  8.83 us
  transfers between devices with their start and end apart: 40, of which 14 were waited for; matrix products, arithmetic and copies ran while one was open for 2% of the time, Pallas kernels for 33%

commit v1 on v0

--- a/solution.py
+++ b/solution.py
@@ -1127,15 +1127,21 @@
         off += n
 
 
-def split_second_body(place_ref, keep, got, kept, sent):
+def split_second_body(sizes, place_ref, *refs):
+    *ins, kept, sent = refs
     _, second, _, _ = spot_of(place_ref)
-
-    def one(z, carry):
-        kept[z] = add(keep[z, second], got[z, second])
-        sent[z] = add(keep[z, 1 - second], got[z, 1 - second])
-        return carry
-
-    lax.fori_loop(0, 4, one, jnp.int32(0))
+    off = 0
+    for i, n in enumerate(sizes):
+        keep, got = ins[2 * i : 2 * i + 2]
+        at = pl.ds(off, n)
+
+        def one(z, carry, keep=keep, got=got, at=at):
+            kept[z, at] = add(keep[z, second], got[z, second])
+            sent[z, at] = add(keep[z, 1 - second], got[z, 1 - second])
+            return carry
+
+        lax.fori_loop(0, 4, one, jnp.int32(0))
+        off += n
 
 
 def split_z_body(plan, place_ref, *refs):
@@ -1149,10 +1155,6 @@
             ref[pl.ds(off, n), :] = add(*terms) if count > 1 else terms[0]
             used += count
             off += n
-
-
-def row_pairs(bit):
-    return [(i, i ^ bit) for i in range(4)]
 
 
 def along(axis):
@@ -1221,21 +1223,23 @@
         self.got = lax.ppermute(sent, ("rows", "tm"), along(0))
         return [self.kept]
 
-    def second(self, deps, work=0):
-        self.kept, sent = call(
-            split_second_body,
-            [SMEM] + [VMEM] * 2,
+
+class Second:
+    def __init__(self, spot, groups, deps):
+        sizes = [group.n for group in groups]
+        self.n = sum(sizes)
+        kept, sent = call(
+            functools.partial(split_second_body, sizes),
+            [SMEM] + [VMEM] * (2 * len(groups)),
             [(struct((4, self.n, LANES), BF), VMEM)] * 2,
             [],
-            (self.spot, self.kept, self.got),
-            moved=3 * self.bytes // 2,
+            (spot, *(v for group in groups for v in (group.kept, group.got))),
+            moved=24 * self.n * LANES * 2,
             name="split_second",
             vmem=VMEM_SMALL,
-            flops=work,
             deps=deps,
         )
-        self.terms = [self.kept, lax.ppermute(sent, ("rows", "tm"), along(1))]
-        return [self.kept]
+        self.terms = [kept, lax.ppermute(sent, ("rows", "tm"), along(1))]
 
 
 def merge_body(*refs):
@@ -1263,8 +1267,7 @@
     mine = lax.psum_scatter(
         part, "tm", scatter_dimension=0, tiled=True, axis_index_groups=[[0, 2, 4, 6], [1, 3, 5, 7]]
     )
-    mine = mine.reshape(part.shape[1:])
-    return mine, lax.all_gather(mine, "rows", axis=0, tiled=True)
+    return mine.reshape(part.shape[1:])
 
 
 def along_z(spot, groups, deps, work=0):
@@ -1308,10 +1311,11 @@
         ins,
         moved=6 * n * LANES,
         name="join",
-        vmem=VMEM_SMALL,
         deps=deps,
     )[0]
-    return [mine] + [lax.ppermute(mine, "rows", row_pairs(bit)) for bit in (1, 2, 3)]
+    one = lax.ppermute(mine, ("rows", "tm"), along(0))
+    two = lax.ppermute(mine, ("rows", "tm"), along(1))
+    return [mine, one, two, lax.ppermute(one, ("rows", "tm"), along(1))]
 
 
 def finish_body(members, by_bit, me_ref, *refs):
@@ -1326,7 +1330,8 @@
     for i, (l, name, n) in enumerate(members):
         for j in range(4):
             if by_bit:
-                owner = pl.multiple_of(jnp.bitwise_xor(me, j) * n, n)
+                flip = (0, 1 + me_ref[1], 2 - me_ref[1], 3)[j]
+                owner = pl.multiple_of(jnp.bitwise_xor(me, flip) * n, n)
                 whole[i, pl.ds(owner, n), :] = chunks[j][pl.ds(off, n), :].astype(F32)
             else:
                 whole[i, pl.ds(j * n, n), :] = chunks[0][pl.ds(j * rows + off, n), :].astype(F32)
@@ -1414,17 +1419,22 @@
     mats = (feed_in, feed_out, attend_in, attend_out, point_in, point_out)
     act, xs, hs, q, kv, at, o, u, z = forward(n, x0, cos, sin, kb, kr, small, mats)
 
-    def unpacked(packed):
-        spread = lax.dot_general(
-            chooser, packed, (((0,), (0,)), ((), ())), preferred_element_type=F32
-        ).astype(BF).reshape(half, 2, 2, frame_count, model_dim)
-        from_below = shifted(spread[:, 0, 1], "tm", 1)
-        from_above = shifted(spread[:, 1, 0], "tm", -1)
-        even = spread[:, 0, 0] + from_below
-        odd = spread[:, 1, 1] + from_above
-        return jnp.stack([even, odd], axis=1).reshape(batches, 1, frame_count, model_dim)
-
-    activations = unpacked(act)
+    def filled(v):
+        return jnp.where(lax.broadcasted_iota(jnp.int32, v.shape, 0) < n[0], v, 0.0).astype(BF)
+
+    def spread(packed):
+        wide = jnp.concatenate(packed, axis=1)
+        frames_of = lax.dot_general(chooser, wide, (((0,), (0,)), ((), ())), preferred_element_type=F32)
+        return frames_of.astype(BF)
+
+    def unpacked(windows_of):
+        windows_of = windows_of.reshape(half, 2, 2, frame_count, 2 * model_dim)
+        from_below = shifted(windows_of[:, 0, 1], "tm", 1)
+        from_above = shifted(windows_of[:, 1, 0], "tm", -1)
+        even = windows_of[:, 0, 0] + from_below
+        odd = windows_of[:, 1, 1] + from_above
+        frames_out = jnp.stack([even, odd], axis=1).reshape(batches, 1, frame_count, 2 * model_dim)
+        return jnp.split(frames_out, 2, axis=-1)
 
     if fast:
         spot = jnp.stack([row % 2, row // 2, tm // 2, tm % 2]).astype(jnp.int32)
@@ -1465,37 +1475,35 @@
         return Group(spot, [(name, members[name][1], crossed[name]) for name in names])
 
     if fast:
-        me = (2 * spot[1] + spot[0]).reshape(1)
+        me = jnp.stack([2 * spot[1] + spot[0], spot[3]])
         back(1, "f1", "c")
         one = group((1, "f1"), (1, "c"))
         made = one.offload([])
         back(1, "a", "f0", deps=made)
+        begin(1, "a")
+        begin(1, "f0")
+        back(0, "f1")
+        begin(0, "f1")
         two = group((1, "a"), (1, "f0"))
-        made = two.offload([])
-        back(0, "f1", deps=made + one.terms)
-        begin(0, "f1")
-        back(0, "c")
+        made = two.offload([g])
+        back(0, "c", deps=made + one.terms)
         begin(0, "c")
         three = group((0, "f1"))
         made = three.first([g])
-        mine_early, all_early = offloaded_rest([one, two], made)
-        back(0, "a", "f0out", deps=made + two.terms)
+        back(0, "a", "f0out", deps=made)
         four = group((0, "c"), (0, "a"), (0, "f0out"))
-        made = three.second([g])
-        made += four.first(made)
-        back(0, "f0in", deps=made + [mine_early], rest=[smalls[name] for name in order[1:]])
+        three_next = Second(spot, [three], [g])
+        made = three_next.terms[:1] + four.first(three_next.terms[:1])
+        z_early = offloaded_rest([one, two], made)
+        back(0, "f0in", deps=made + two.terms, rest=[smalls[name] for name in order[1:]])
         five = group((0, "f0in"))
-        z_three = along_z(spot, [three], [g], TAIL_WORK)
+        z_three = along_z(spot, [three_next], [g, four.got], TAIL_WORK)
         made = five.first(z_three[:1])
-        made = four.second(made)
-        z_four = along_z(spot, [four], made)
-        made = five.second(z_four[:1])
-        outs = finish(layers, me, [one, two], [all_early], [], made)
-        chunks_mid = gathered([z_three, z_four], outs[:1])
-        z_five = along_z(spot, [five], chunks_mid[:1])
-        outs = finish(layers, me, [three, four], chunks_mid, outs)
-        chunks_late = gathered([z_five], outs[:1])
-        *mats_out, small_out = finish(layers, me, [five], chunks_late, outs)
+        last = Second(spot, [four, five], made)
+        z_last = along_z(spot, [last], z_three[1:])
+        home = spread([act, filled(g)])
+        chunks = gathered([[z_early], z_three, z_last], [home])
+        *mats_out, small_out = finish(layers, me, [one, two, three, four, five], chunks, [])
         mats_out = [
             v.swapaxes(-1, -2) if turned else v for v, turned in zip(mats_out, (False, True, True, True, False, True))
         ]
@@ -1514,8 +1522,8 @@
             back(l, "f1", "c")
             back(l, "a", "f0")
         pieces = None
-    filled = lax.broadcasted_iota(jnp.int32, g.shape, 0) < n[0]
-    frames_grad = unpacked(jnp.where(filled, g, 0.0).astype(BF))
+        home = spread([act, filled(g)])
+    activations, frames_grad = unpacked(home)
 
     if not fast:
         mats_out, lines_of = general_sums(layers, members, smalls, order)

time: 373 us -> 366 us (0.981)
  local copies, waits for them, and re-layouts: 36 us -> 22.4 us
  starting transfers between devices: 43.2 us -> 31.7 us
  waiting for transfers between devices: 57.3 us -> 67.7 us
  Pallas kernels: 209 us -> 215 us
    ppermute x3, waiting for transfers between devices: 0.01 us -> 16 us  [first(): self.got = lax.ppermute(sent, ('rows', 'tm'), along(0))]
    unnamed x94 -> x82, local copies, waits for them, and re-layouts: 29.6 us -> 17.2 us
    ppermute x9 -> x6, waiting for transfers between devices: 11.5 us -> 23.9 us  [along_z(): lax.ppermute(v, 'tm', [(i, (i + 2 * k) % 8) for i in range(8)])]
    pallas_call x22 -> x19, Pallas kernels: 202 us -> 210 us  [call(): pl.pallas_call(inner, out_shape=[s for s, _ in outs], in_specs=list(ins)...]
    unnamed x6 -> x5, waiting for transfers between devices: 7.64 us -> 0.05 us
    ppermute x9 -> x5, waiting for transfers between devices: 20.4 us -> 13.6 us  [the longest x1 7.49 us: gathered(): return [mine, one, two, lax.ppermute(one, ('rows', 'tm'), along(1))]]
    ppermute x6 -> x4, starting transfers between devices: 15.4 us -> 9.88 us  [shifted(): return lax.ppermute(array, axis, pairs)]
    ppermute x9 -> x5, starting transfers between devices: 10.4 us -> 6.74 us  [the longest x2 2.66 us: __init__(): self.terms = [kept, lax.ppermute(sent, ('rows', 'tm'), along(1))]]
  transfers between devices with their start and end apart: 40 -> 30, of which waited for: 14 -> 15; matrix products, arithmetic and copies ran while one was open for 2% -> 3% of each run, Pallas kernels for 33% -> 34%
where the time goes in v1:
time: 366 us; the launch traced here: 360 us
  Pallas kernels  215 us (59%)
  waiting for transfers between devices  67.7 us (18%)
  starting transfers between devices  31.7 us (9%)
  local copies, waits for them, and re-layouts  22.4 us (6%)
  between operations  14.5 us (4%)
  other arithmetic  4.76 us (1%)
  matrix products  3.76 us (1%)
    pallas_call x19, Pallas kernels, call(): pl.pallas_call(inner, out_shape=[s for s, _ in outs], in_specs=list(ins)...  210 us
    ppermute x6, waiting for transfers between devices, along_z(): lax.ppermute(v, 'tm', [(i, (i + 2 * k) % 8) for i in range(8)])  23.9 us
    unnamed x82, local copies, waits for them, and re-layouts  17.2 us
    ppermute x3, waiting for transfers between devices, first(): self.got = lax.ppermute(sent, ('rows', 'tm'), along(0))  16 us
    ppermute x4, starting transfers between devices, shifted(): return lax.ppermute(array, axis, pairs)  9.88 us
    ppermute x6, starting transfers between devices, along_z(): lax.ppermute(v, 'tm', [(i, (i + 2 * k) % 8) for i in range(8)])  9.23 us
    ppermute x1, waiting for transfers between devices, gathered(): return [mine, one, two, lax.ppermute(one, ('rows', 'tm'), along(1))]  7.49 us
  transfers between devices with their start and end apart: 30, of which 15 were waited for; matrix products, arithmetic and copies ran while one was open for 3% of the time, Pallas kernels for 34%

profile of v1, /device:TPU:10, one launch (start us, length us, event | category | flops | bytes accessed | tf_op | source)
XLA Modules:
  0.0 359.8 jit_solution(13535228179239603826)
XLA Ops:
  12.7 2.4 collective-permute-start
  16.4 3.2 collective-permute-done.1.refs_4_
  19.5 3.8 %collective-permute-done.refs_3_ = bf16[528,512]{1,0:T(8,128)(2,1)S(1)} collective-permute-done((bf16[528,512]{1,0:T(8,128)(2,1)S(1)}, bf16[528,512]{1,0:T(8,128)(2,1)S(1)}, u32[]{:S(2)}, u32[]{:S(2)}) %collective-permute-start) | collective-permute-done | bytes 540704 | tf_op jit(solution)/shard_map/ppermute | solution.py:37
  24.1 7.5 %pack.1 = (f32[1024,512]{1,0:T(8,128)}, f32[1024,512]{1,0:T(8,128)}, bf16[1024,1024]{1,0:T(8,128)(2,1)}, f32[1024,128]{1,0:T(8,128)}, f32[1024,128]{1,0:T(8,128)...) custom-call(f32[4,128]{1,0:T(4,128)} %get-tuple-element.209.refs_0_, bf16[512,512]{1,0:T(8,128)(2,1)} %bitcast.119, ...), custom_call_target="tpu_custom_call" | custom-call | flops 2147483648 | bytes 12582912 | tf_op jit(solution)/shard_map/pack/pallas_call | solution.py:50
  31.6 42.6 %forward.1 = (bf16[1024,512]{1,0:T(8,128)(2,1)}, f32[2,5,1024,512]{3,2,1,0:T(8,128)}, bf16[2,2,1024,2048]{3,2,1,0:T(8,128)(2,1)}, bf16[2,1024,512]{2,1,0:T(8,128...) custom-call(s32[1]{0:T(128)} %get-tuple-element.86.refs_0_, ...), custom_call_target="tpu_custom_call" | custom-call | flops 15360000000 | bytes 62914560 | tf_op jit(solution)/shard_map/forward/pallas_call | solution.py:50
  74.2 32.4 %back_1_f1_c.1 = (f32[1024,512]{1,0:T(8,128)}, bf16[4,1024,256]{2,1,0:T(8,128)(2,1)}, bf16[4,1024,256]{2,1,0:T(8,128)(2,1)}, f32[8,512]{1,0:T(8,128)}, bf16[4,38...) custom-call(s32[1]{0:T(128)} %get-tuple-element.86.refs_0_, s32[1]{0:T(128)} %bitcast.12.refs_1_, ...), custom_call_target="tpu_custom_call" | custom-call | flops 7381975040 | bytes 16777216 | tf_op jit(solution)/shard_map/back_1_f1_c/pallas_call | solution.py:50
  107.2 5.0 %collective-permute-done.3 = bf16[4,384,256]{2,1,0:T(8,128)(2,1)S(1)} collective-permute-done((bf16[4,384,256]{2,1,0:T(8,128)(2,1)}, bf16[4,384,256]{2,1,0:T(8,128)(2,1)S(1)}, u32[]{:S(2)}, u32[]{:S(2)}) %collective-permute-start.3) | collective-permute-done | bytes 786464 | tf_op jit(solution)/shard_map/ppermute | solution.py:1469
  114.9 2.3 sum_cores.2.refs_18_
  117.3 32.1 %back_1_a_f0.1 = (f32[1024,512]{1,0:T(8,128)}, bf16[4,512,256]{2,1,0:T(8,128)(2,1)}, bf16[4,512,256]{2,1,0:T(8,128)(2,1)}, f32[8,512]{1,0:T(8,128)}, bf16[4,1024...) custom-call(s32[1]{0:T(128)} %get-tuple-element.86.refs_0_, s32[1]{0:T(128)} %bitcast.12.refs_1_, ...), custom_call_target="tpu_custom_call" | custom-call | flops 8053063680 | bytes 16777216 | tf_op jit(solution)/shard_map/back_1_a_f0/pallas_call | solution.py:50
  149.9 20.4 %back_0_f1.1 = (f32[1024,512]{1,0:T(8,128)}, bf16[4,1024,256]{2,1,0:T(8,128)(2,1)}, bf16[4,1024,256]{2,1,0:T(8,128)(2,1)}, f32[8,512]{1,0:T(8,128)}) custom-call(s32[1]{0:T(128)} %get-tuple-element.86.refs_0_, s32[1]{0:T(128)} %bitcast.12.refs_1_, f32[1024,512]{1,0:T(8,128)} %get-tuple-element.107.refs_2_, ...), custom_call_target="tpu_custom_call" | custom-call | flops 5368709120 | bytes 16777216 | tf_op jit(solution)/shard_map/back_0_f1/pallas_call | solution.py:50
  172.0 4.3 %sum_cores.3.refs_15_ = bf16[4,4,384,256]{3,2,1,0:T(8,128)(2,1)} custom-call(bf16[4,4,128,256]{3,2,1,0:T(8,128)(2,1)S(1)} %bitcast.106, bf16[4,4,256,256]{3,2,1,0:T(8,128)(2,1)S(1)} %bitcast.97, bf16[4,4,128,256]{3,2,1,0:T(8,128)(2,1)} %bitcast.19.refs_2_, bf16[4,4,256,256]{3,2,1,0:T(8,128)(2,1)} %bitcast.20.refs_3_, f32[1024,512]{1,0:T(8,128)S(1)} %copy-done.4), custom_call_target="tpu_custom_call" | custom-call | bytes 9437184 | tf_op jit(solution)/shard_map/sum_cores/pallas_call | solution.py:50
  176.7 15.0 %back_0_c.1 = (f32[1024,512]{1,0:T(8,128)}, bf16[4,384,256]{2,1,0:T(8,128)(2,1)}, bf16[4,384,256]{2,1,0:T(8,128)(2,1)}, f32[24,512]{1,0:T(8,128)}) custom-call(s32[1]{0:T(128)} %get-tuple-element.86.refs_0_, s32[1]{0:T(128)} %bitcast.12.refs_1_, f32[1024,512]{1,0:T(8,128)} %get-tuple-element.108.refs_4_.refs_2_, ...), custom_call_target="tpu_custom_call" | custom-call | flops 2013265920 | bytes 16777216 | tf_op jit(solution)/shard_map/back_0_c/pallas_call | solution.py:50
  193.4 3.3 split_first.3
  198.2 24.9 %back_0_a_f0out.1 = (f32[1024,512]{1,0:T(8,128)}, bf16[4,512,256]{2,1,0:T(8,128)(2,1)}, bf16[4,512,256]{2,1,0:T(8,128)(2,1)}, f32[8,512]{1,0:T(8,128)}, bf16[4,5...) custom-call(s32[1]{0:T(128)} %get-tuple-element.86.refs_0_, s32[1]{0:T(128)} %bitcast.12.refs_1_, ...), custom_call_target="tpu_custom_call" | custom-call | flops 4026531840 | bytes 16777216 | tf_op jit(solution)/shard_map/back_0_a_f0out/pallas_call | solution.py:50
  227.4 2.2 collective-permute-done.8
  229.7 2.4 split_first.4
  236.5 13.2 %back_0_f0in.1 = (f32[1024,512]{1,0:T(8,128)}, bf16[4,640,256]{2,1,0:T(8,128)(2,1)}, bf16[4,640,256]{2,1,0:T(8,128)(2,1)}, f32[8,512]{1,0:T(8,128)}) custom-call(s32[1]{0:T(128)} %get-tuple-element.86.refs_0_, s32[1]{0:T(128)} %bitcast.12.refs_1_, f32[1024,512]{1,0:T(8,128)} %get-tuple-element.117.refs_3_.refs_2_, ...), custom_call_target="tpu_custom_call" | custom-call | flops 4026531840 | bytes 16777216 | tf_op jit(solution)/shard_map/back_0_f0in/pallas_call | solution.py:50
  249.9 6.6 %collective-permute-done.14.refs_4_.refs_2_ = bf16[4,2,352,256]{3,2,1,0:T(8,128)(2,1)} collective-permute-done((bf16[4,2,352,256]{3,2,1,0:T(8,128)(2,1)}, bf16[4,2,352,256]{3,2,1,0:T(8,128)(2,1)}, u32[]{:S(2)}, u32[]{:S(2)}) %collective-permute-start.14) | collective-permute-done | bytes 1441824 | tf_op jit(solution)/shard_map/ppermute | solution.py:1223
  261.7 9.4 %collective-permute-done.19.refs_4_ = bf16[4,2,160,256]{3,2,1,0:T(8,128)(2,1)S(1)} collective-permute-done((bf16[4,2,160,256]{3,2,1,0:T(8,128)(2,1)S(1)}, bf16[4,2,160,256]{3,2,1,0:T(8,128)(2,1)S(1)}, u32[]{:S(2)}, u32[]{:S(2)}) %collective-permute-start.19) | collective-permute-done | bytes 655392 | tf_op jit(solution)/shard_map/ppermute | solution.py:1223
  271.1 2.0 split_second.3
  277.9 1.9 collective-permute-start.17
  280.1 4.9 %collective-permute-done.15.refs_3_.refs_2_ = bf16[256,256]{1,0:T(8,128)(2,1)S(1)} collective-permute-done((bf16[256,256]{1,0:T(8,128)(2,1)S(1)}, bf16[256,256]{1,0:T(8,128)(2,1)S(1)}, u32[]{:S(2)}, u32[]{:S(2)}) %collective-permute-start.15) | collective-permute-done | bytes 131104 | tf_op jit(solution)/shard_map/ppermute | solution.py:1289
  292.1 2.2 collective-permute-start.23
  294.3 3.8 %fusion.4.refs_9_ = bf16[1024,1024]{1,0:T(8,128)(2,1)} fusion(bf16[1024,1024]{1,0:T(8,128)(2,1)S(1)} %copy-done.37, bf16[1024,512]{1,0:T(8,128)(2,1)S(1)} %select_convert_fusion, bf16[1024,512]{1,0:T(8,128)(2,1)S(1)} %copy-done.38), kind=kOutput, calls=%fused_computation.5 | convolution fusion | flops 2152726528 | bytes 6291456 | tf_op jit(solution)/shard_map/dot_general | solution.py:1427
  298.1 11.0 %collective-permute-done.21.refs_6_ = bf16[512,256]{1,0:T(8,128)(2,1)S(1)} collective-permute-done((bf16[512,256]{1,0:T(8,128)(2,1)S(1)}, bf16[512,256]{1,0:T(8,128)(2,1)S(1)}, u32[]{:S(2)}, u32[]{:S(2)}) %collective-permute-start.21) | collective-permute-done | bytes 262176 | tf_op jit(solution)/shard_map/ppermute | solution.py:1289
  309.1 3.4 collective-permute-done.22.refs_7_
  314.6 2.7 join.1.refs_1_
  321.7 3.6 %collective-permute-start.12 = (bf16[2,128,1024]{2,1,0:T(8,128)(2,1)}, bf16[2,128,1024]{2,1,0:T(8,128)(2,1)}, u32[]{:S(2)}, u32[]{:S(2)}) collective-permute-start(bf16[2,128,1024]{2,1,0:T(8,128)(2,1)} %get-tuple-element.185), channel_id=1, source_target_pairs={{1,0},{2,1},{3,2},{4,3},{5,4},{6,5},{7,6},{9,8},{10,9},{11,10},{12... | collective-permute-start | bytes 1572872 | tf_op jit(solution)/shard_map/ppermute | solution.py:37
  325.9 6.1 %collective-permute-done.24.refs_2_ = bf16[1504,256]{1,0:T(8,128)(2,1)} collective-permute-done((bf16[1504,256]{1,0:T(8,128)(2,1)}, bf16[1504,256]{1,0:T(8,128)(2,1)}, u32[]{:S(2)}, u32[]{:S(2)}) %collective-permute-start.24) | collective-permute-done | bytes 770080 | tf_op jit(solution)/shard_map/ppermute | solution.py:1316
  331.9 2.1 collective-permute-start.26
  338.1 7.5 %collective-permute-done.26.refs_4_ = bf16[1504,256]{1,0:T(8,128)(2,1)} collective-permute-done((bf16[1504,256]{1,0:T(8,128)(2,1)}, bf16[1504,256]{1,0:T(8,128)(2,1)}, u32[]{:S(2)}, u32[]{:S(2)}) %collective-permute-start.26) | collective-permute-done | bytes 770080 | tf_op jit(solution)/shard_map/ppermute | solution.py:1318
  345.6 4.7 %finish.1 = (f32[2,2,512,256]{3,2,1,0:T(8,128)}, f32[2,2,64,2048]{3,2,1,0:T(8,128)}, f32[2,192,512]{2,1,0:T(8,128)}, f32[2,64,512]{2,1,0:T(8,128)}, f32[2,512,12...) custom-call(s32[2]{0:T(128)} %pad_add_fusion.1.refs_0_, bf16[1504,256]{1,0:T(8,128)(2,1)} %join.1.refs_1_, ...), custom_call_target="tpu_custom_call" | custom-call | tf_op jit(solution)/shard_map/finish/pallas_call | solution.py:1382
  (157 shorter events, 56.3 us)
Async XLA Ops:
  7.2 169.5 %reduce-scatter.10.cloned.1.call-start = ((), (), s32[]{:S(2)}) async-start(), calls=%async_computation.4 | async-start | bytes 3604480
  10.7 8.8 %collective-permute-start.1 = (bf16[528,512]{1,0:T(8,128)(2,1)S(1)}, bf16[528,512]{1,0:T(8,128)(2,1)S(1)}, u32[]{:S(2)}, u32[]{:S(2)}) collective-permute-start(bf16[528,512]{1,0:T(8,128)(2,1)S(1)} %get-tuple-element.206), channel_id=1, source_target_pairs={{1,0},{2,1},{3,2},{4,3},{5,4},{6,5},{7,6},{9,8},{10,9},{11,10},{12... | collective-permute-start | bytes 1622024 | tf_op jit(solution)/shard_map/ppermute | solution.py:37
  12.7 10.7 %collective-permute-start = (bf16[528,512]{1,0:T(8,128)(2,1)S(1)}, bf16[528,512]{1,0:T(8,128)(2,1)S(1)}, u32[]{:S(2)}, u32[]{:S(2)}) collective-permute-start(bf16[528,512]{1,0:T(8,128)(2,1)S(1)} %get-tuple-element.207), channel_id=1, source_target_pairs={{0,1},{1,2},{2,3},{3,4},{4,5},{5,6},{6,7},{8,9},{9,10},{10,11},{11... | collective-permute-start | bytes 1622024 | tf_op jit(solution)/shard_map/ppermute | solution.py:37
  106.6 5.6 %collective-permute-start.2 = (bf16[4,1024,256]{2,1,0:T(8,128)(2,1)}, bf16[4,1024,256]{2,1,0:T(8,128)(2,1)S(1)}, u32[]{:S(2)}, u32[]{:S(2)}) collective-permute-start(bf16[4,1024,256]{2,1,0:T(8,128)(2,1)} %get-tuple-element.105), channel_id=1, source_target_pairs={{0,1},{1,0},{2,3},{3,2},{4,5},{5,4},{6,7},{7,6},{8,9},{9,8},{10,11... | collective-permute-start | bytes 6291464 | tf_op jit(solution)/shard_map/ppermute | solution.py:1469
  106.7 5.5 %collective-permute-start.3 = (bf16[4,384,256]{2,1,0:T(8,128)(2,1)}, bf16[4,384,256]{2,1,0:T(8,128)(2,1)S(1)}, u32[]{:S(2)}, u32[]{:S(2)}) collective-permute-start(bf16[4,384,256]{2,1,0:T(8,128)(2,1)} %get-tuple-element.106), channel_id=1, source_target_pairs={{0,1},{1,0},{2,3},{3,2},{4,5},{5,4},{6,7},{7,6},{8,9},{9,8},{10,11... | collective-permute-start | bytes 2359304 | tf_op jit(solution)/shard_map/ppermute | solution.py:1469
  117.2 116.9 %reduce-scatter.12.cloned.1.call-start = ((), (), s32[]{:S(2)}) async-start(), calls=%async_computation.5 | async-start | bytes 3932160
  149.3 21.0 %collective-permute-start.5 = (bf16[4,1024,256]{2,1,0:T(8,128)(2,1)}, bf16[4,1024,256]{2,1,0:T(8,128)(2,1)}, u32[]{:S(2)}, u32[]{:S(2)}) collective-permute-start(bf16[4,1024,256]{2,1,0:T(8,128)(2,1)} %get-tuple-element.112), channel_id=1, source_target_pairs={{0,1},{1,0},{2,3},{3,2},{4,5},{5,4},{6,7},{7,6},{8,9},{9,8},{10,11... | collective-permute-start | bytes 6291464 | tf_op jit(solution)/shard_map/ppermute | solution.py:1469
  149.5 20.9 %collective-permute-start.4 = (bf16[4,512,256]{2,1,0:T(8,128)(2,1)}, bf16[4,512,256]{2,1,0:T(8,128)(2,1)}, u32[]{:S(2)}, u32[]{:S(2)}) collective-permute-start(bf16[4,512,256]{2,1,0:T(8,128)(2,1)} %get-tuple-element.111), channel_id=1, source_target_pairs={{0,1},{1,0},{2,3},{3,2},{4,5},{5,4},{6,7},{7,6},{8,9},{9,8},{10,11... | collective-permute-start | bytes 3145736 | tf_op jit(solution)/shard_map/ppermute | solution.py:1469
  149.9 20.5 %copy-start.19 = (bf16[4,512,256]{2,1,0:T(8,128)(2,1)S(1)}, bf16[4,512,256]{2,1,0:T(8,128)(2,1)}, u32[]{:S(2)}) copy-start(bf16[4,512,256]{2,1,0:T(8,128)(2,1)} %get-tuple-element.109) | copy-start | bytes 3145732
  176.3 121.7 %reduce-scatter.8.cloned.1.call-start = ((), (), s32[]{:S(2)}) async-start(), calls=%async_computation.3 | async-start | bytes 1884160 | tf_op jit(solution)/shard_map/reduce_scatter | solution.py:1267
  176.4 15.2 %collective-permute-start.6 = (bf16[4,1024,256]{2,1,0:T(8,128)(2,1)}, bf16[4,1024,256]{2,1,0:T(8,128)(2,1)}, u32[]{:S(2)}, u32[]{:S(2)}) collective-permute-start(bf16[4,1024,256]{2,1,0:T(8,128)(2,1)} %get-tuple-element.115), channel_id=1, source_target_pairs={{0,1},{1,0},{2,3},{3,2},{4,5},{5,4},{6,7},{7,6},{8,9},{9,8},{10,11... | collective-permute-start | bytes 6291464 | tf_op jit(solution)/shard_map/ppermute | solution.py:1469
  197.7 27.3 %collective-permute-start.7 = (bf16[4,2,256,256]{3,2,1,0:T(8,128)(2,1)}, bf16[4,2,256,256]{3,2,1,0:T(8,128)(2,1)S(1)}, u32[]{:S(2)}, u32[]{:S(2)}) collective-permute-start(bf16[4,2,256,256]{3,2,1,0:T(8,128)(2,1)} %get-tuple-element.125), channel_id=1, source_target_pairs={{0,8},{1,17},{2,10},{3,19},{4,12},{5,21},{6,14},{7,23},{8,0},{9,25... | collective-permute-start | bytes 3145736 | tf_op jit(solution)/shard_map/ppermute | solution.py:1223
  198.2 26.8 %copy-start.8 = (bf16[4,2,256,256]{3,2,1,0:T(8,128)(2,1)S(1)}, bf16[4,2,256,256]{3,2,1,0:T(8,128)(2,1)}, u32[]{:S(2)}) copy-start(bf16[4,2,256,256]{3,2,1,0:T(8,128)(2,1)} %copy-done.7) | copy-start | bytes 3145732
  223.2 6.4 %collective-permute-start.9 = (bf16[4,512,256]{2,1,0:T(8,128)(2,1)}, bf16[4,512,256]{2,1,0:T(8,128)(2,1)S(1)}, u32[]{:S(2)}, u32[]{:S(2)}) collective-permute-start(bf16[4,512,256]{2,1,0:T(8,128)(2,1)} %get-tuple-element.131), channel_id=1, source_target_pairs={{0,1},{1,0},{2,3},{3,2},{4,5},{5,4},{6,7},{7,6},{8,9},{9,8},{10,11... | collective-permute-start | bytes 3145736 | tf_op jit(solution)/shard_map/ppermute | solution.py:1469
  224.5 5.1 %collective-permute-start.10 = (bf16[4,512,256]{2,1,0:T(8,128)(2,1)}, bf16[4,512,256]{2,1,0:T(8,128)(2,1)S(1)}, u32[]{:S(2)}, u32[]{:S(2)}) collective-permute-start(bf16[4,512,256]{2,1,0:T(8,128)(2,1)} %get-tuple-element.132), channel_id=1, source_target_pairs={{0,1},{1,0},{2,3},{3,2},{4,5},{5,4},{6,7},{7,6},{8,9},{9,8},{10,11... | collective-permute-start | bytes 3145736 | tf_op jit(solution)/shard_map/ppermute | solution.py:1469
  224.6 5.0 %collective-permute-start.8 = (bf16[4,384,256]{2,1,0:T(8,128)(2,1)}, bf16[4,384,256]{2,1,0:T(8,128)(2,1)S(1)}, u32[]{:S(2)}, u32[]{:S(2)}) collective-permute-start(bf16[4,384,256]{2,1,0:T(8,128)(2,1)} %get-tuple-element.130), channel_id=1, source_target_pairs={{0,1},{1,0},{2,3},{3,2},{4,5},{5,4},{6,7},{7,6},{8,9},{9,8},{10,11... | collective-permute-start | bytes 2359304 | tf_op jit(solution)/shard_map/ppermute | solution.py:1469
  232.1 24.4 %collective-permute-start.14 = (bf16[4,2,352,256]{3,2,1,0:T(8,128)(2,1)}, bf16[4,2,352,256]{3,2,1,0:T(8,128)(2,1)}, u32[]{:S(2)}, u32[]{:S(2)}) collective-permute-start(bf16[4,2,352,256]{3,2,1,0:T(8,128)(2,1)} %get-tuple-element.136), channel_id=1, source_target_pairs={{0,8},{1,17},{2,10},{3,19},{4,12},{5,21},{6,14},{7,23},{8,0},{9,25... | collective-permute-start | bytes 4325384 | tf_op jit(solution)/shard_map/ppermute | solution.py:1223
  232.8 17.0 %collective-permute-start.13 = (bf16[4,256,256]{2,1,0:T(8,128)(2,1)S(1)}, bf16[4,256,256]{2,1,0:T(8,128)(2,1)}, u32[]{:S(2)}, u32[]{:S(2)}) collective-permute-start(bf16[4,256,256]{2,1,0:T(8,128)(2,1)S(1)} %get-tuple-element.135), channel_id=1, source_target_pairs={{0,16},{1,9},{2,18},{3,11},{4,20},{5,13},{6,22},{7,15},{8,24},{9,1... | collective-permute-start | bytes 1572872 | tf_op jit(solution)/shard_map/ppermute | solution.py:1242
  249.8 9.6 %collective-permute-start.18 = (bf16[4,640,256]{2,1,0:T(8,128)(2,1)}, bf16[4,640,256]{2,1,0:T(8,128)(2,1)S(1)}, u32[]{:S(2)}, u32[]{:S(2)}) collective-permute-start(bf16[4,640,256]{2,1,0:T(8,128)(2,1)} %get-tuple-element.142), channel_id=1, source_target_pairs={{0,1},{1,0},{2,3},{3,2},{4,5},{5,4},{6,7},{7,6},{8,9},{9,8},{10,11... | collective-permute-start | bytes 3932168 | tf_op jit(solution)/shard_map/ppermute | solution.py:1469
  260.4 10.7 %collective-permute-start.19 = (bf16[4,2,160,256]{3,2,1,0:T(8,128)(2,1)S(1)}, bf16[4,2,160,256]{3,2,1,0:T(8,128)(2,1)S(1)}, u32[]{:S(2)}, u32[]{:S(2)}) collective-permute-start(bf16[4,2,160,256]{3,2,1,0:T(8,128)(2,1)S(1)} %get-tuple-element.144), channel_id=1, source_target_pairs={{0,8},{1,17},{2,10},{3,19},{4,12},{5,21},{6,14},{7,23},{8,0},{9,25... | collective-permute-start | bytes 1966088 | tf_op jit(solution)/shard_map/ppermute | solution.py:1223
  273.2 15.0 %collective-permute-start.20 = (bf16[4,512,256]{2,1,0:T(8,128)(2,1)S(1)}, bf16[4,512,256]{2,1,0:T(8,128)(2,1)S(1)}, u32[]{:S(2)}, u32[]{:S(2)}) collective-permute-start(bf16[4,512,256]{2,1,0:T(8,128)(2,1)S(1)} %get-tuple-element.146), channel_id=1, source_target_pairs={{0,16},{1,9},{2,18},{3,11},{4,20},{5,13},{6,22},{7,15},{8,24},{9,1... | collective-permute-start | bytes 3145736 | tf_op jit(solution)/shard_map/ppermute | solution.py:1242
  275.2 9.7 %collective-permute-start.15 = (bf16[256,256]{1,0:T(8,128)(2,1)S(1)}, bf16[256,256]{1,0:T(8,128)(2,1)S(1)}, u32[]{:S(2)}, u32[]{:S(2)}) collective-permute-start(bf16[256,256]{1,0:T(8,128)(2,1)S(1)} %get-tuple-element.138), channel_id=1, source_target_pairs={{0,2},{1,3},{2,4},{3,5},{4,6},{5,7},{6,0},{7,1},{8,10},{9,11},{10,... | collective-permute-start | bytes 393224 | tf_op jit(solution)/shard_map/ppermute | solution.py:1289
  276.8 9.5 %collective-permute-start.16 = (bf16[256,256]{1,0:T(8,128)(2,1)S(1)}, bf16[256,256]{1,0:T(8,128)(2,1)S(1)}, u32[]{:S(2)}, u32[]{:S(2)}) collective-permute-start(bf16[256,256]{1,0:T(8,128)(2,1)S(1)} %get-tuple-element.139), channel_id=1, source_target_pairs={{0,4},{1,5},{2,6},{3,7},{4,0},{5,1},{6,2},{7,3},{8,12},{9,13},{10,... | collective-permute-start | bytes 393224 | tf_op jit(solution)/shard_map/ppermute | solution.py:1289
  277.9 10.3 %collective-permute-start.17 = (bf16[256,256]{1,0:T(8,128)(2,1)S(1)}, bf16[256,256]{1,0:T(8,128)(2,1)S(1)}, u32[]{:S(2)}, u32[]{:S(2)}) collective-permute-start(bf16[256,256]{1,0:T(8,128)(2,1)S(1)} %get-tuple-element.140), channel_id=1, source_target_pairs={{0,6},{1,7},{2,0},{3,1},{4,2},{5,3},{6,4},{7,5},{8,14},{9,15},{10,... | collective-permute-start | bytes 393224 | tf_op jit(solution)/shard_map/ppermute | solution.py:1289
  289.7 19.4 %collective-permute-start.21 = (bf16[512,256]{1,0:T(8,128)(2,1)S(1)}, bf16[512,256]{1,0:T(8,128)(2,1)S(1)}, u32[]{:S(2)}, u32[]{:S(2)}) collective-permute-start(bf16[512,256]{1,0:T(8,128)(2,1)S(1)} %get-tuple-element.148), channel_id=1, source_target_pairs={{0,2},{1,3},{2,4},{3,5},{4,6},{5,7},{6,0},{7,1},{8,10},{9,11},{10,... | collective-permute-start | bytes 786440 | tf_op jit(solution)/shard_map/ppermute | solution.py:1289
  291.1 21.4 %collective-permute-start.22 = (bf16[512,256]{1,0:T(8,128)(2,1)S(1)}, bf16[512,256]{1,0:T(8,128)(2,1)S(1)}, u32[]{:S(2)}, u32[]{:S(2)}) collective-permute-start(bf16[512,256]{1,0:T(8,128)(2,1)S(1)} %get-tuple-element.149), channel_id=1, source_target_pairs={{0,4},{1,5},{2,6},{3,7},{4,0},{5,1},{6,2},{7,3},{8,12},{9,13},{10,... | collective-permute-start | bytes 786440 | tf_op jit(solution)/shard_map/ppermute | solution.py:1289
  292.1 21.8 %collective-permute-start.23 = (bf16[512,256]{1,0:T(8,128)(2,1)S(1)}, bf16[512,256]{1,0:T(8,128)(2,1)S(1)}, u32[]{:S(2)}, u32[]{:S(2)}) collective-permute-start(bf16[512,256]{1,0:T(8,128)(2,1)S(1)} %get-tuple-element.150), channel_id=1, source_target_pairs={{0,6},{1,7},{2,0},{3,1},{4,2},{5,3},{6,4},{7,5},{8,14},{9,15},{10,... | collective-permute-start | bytes 786440 | tf_op jit(solution)/shard_map/ppermute | solution.py:1289
  317.3 14.6 %collective-permute-start.24 = (bf16[1504,256]{1,0:T(8,128)(2,1)}, bf16[1504,256]{1,0:T(8,128)(2,1)}, u32[]{:S(2)}, u32[]{:S(2)}) collective-permute-start(bf16[1504,256]{1,0:T(8,128)(2,1)} %join.1.refs_1_), channel_id=1, source_target_pairs={{0,8},{1,17},{2,10},{3,19},{4,12},{5,21},{6,14},{7,23},{8,0},{9,25... | collective-permute-start | bytes 2310152 | tf_op jit(solution)/shard_map/ppermute | solution.py:1316
  319.8 14.9 %collective-permute-start.11 = (bf16[2,128,1024]{2,1,0:T(8,128)(2,1)}, bf16[2,128,1024]{2,1,0:T(8,128)(2,1)S(1)}, u32[]{:S(2)}, u32[]{:S(2)}) collective-permute-start(bf16[2,128,1024]{2,1,0:T(8,128)(2,1)} %get-tuple-element.184), channel_id=1, source_target_pairs={{0,1},{1,2},{2,3},{3,4},{4,5},{5,6},{6,7},{8,9},{9,10},{10,11},{11... | collective-permute-start | bytes 1572872 | tf_op jit(solution)/shard_map/ppermute | solution.py:37
  321.7 13.0 %collective-permute-start.12 = (bf16[2,128,1024]{2,1,0:T(8,128)(2,1)}, bf16[2,128,1024]{2,1,0:T(8,128)(2,1)}, u32[]{:S(2)}, u32[]{:S(2)}) collective-permute-start(bf16[2,128,1024]{2,1,0:T(8,128)(2,1)} %get-tuple-element.185), channel_id=1, source_target_pairs={{1,0},{2,1},{3,2},{4,3},{5,4},{6,5},{7,6},{9,8},{10,9},{11,10},{12... | collective-permute-start | bytes 1572872 | tf_op jit(solution)/shard_map/ppermute | solution.py:37
  325.3 11.9 %collective-permute-start.25 = (bf16[1504,256]{1,0:T(8,128)(2,1)S(1)}, bf16[1504,256]{1,0:T(8,128)(2,1)S(1)}, u32[]{:S(2)}, u32[]{:S(2)}) collective-permute-start(bf16[1504,256]{1,0:T(8,128)(2,1)S(1)} %copy-done.28), channel_id=1, source_target_pairs={{0,16},{1,9},{2,18},{3,11},{4,20},{5,13},{6,22},{7,15},{8,24},{9,1... | collective-permute-start | bytes 2310152 | tf_op jit(solution)/shard_map/ppermute | solution.py:1317
  331.9 13.6 %collective-permute-start.26 = (bf16[1504,256]{1,0:T(8,128)(2,1)}, bf16[1504,256]{1,0:T(8,128)(2,1)}, u32[]{:S(2)}, u32[]{:S(2)}) collective-permute-start(bf16[1504,256]{1,0:T(8,128)(2,1)} %collective-permute-done.24.refs_2_), channel_id=1, source_target_pairs={{0,16},{1,9},{2,18},{3,11},{4,20},{5,13},{6,22},{7,15},{8,24},{9,1... | collective-permute-start | bytes 2310152 | tf_op jit(solution)/shard_map/ppermute | solution.py:1318
  (37 other events, 233.8 us)
Sparse Core Ops, SparseCore 0:
  117.3 42.8 reduce-scatter.9
  176.5 47.7 reduce-scatter.11
  236.6 32.8 reduce-scatter.7

commit v2 on v1

--- a/solution.py
+++ b/solution.py
@@ -1427,10 +1427,12 @@
         frames_of = lax.dot_general(chooser, wide, (((0,), (0,)), ((), ())), preferred_element_type=F32)
         return frames_of.astype(BF)
 
-    def unpacked(windows_of):
+    def crossing(windows_of):
         windows_of = windows_of.reshape(half, 2, 2, frame_count, 2 * model_dim)
-        from_below = shifted(windows_of[:, 0, 1], "tm", 1)
-        from_above = shifted(windows_of[:, 1, 0], "tm", -1)
+        return [shifted(windows_of[:, 0, 1], "tm", 1), shifted(windows_of[:, 1, 0], "tm", -1)]
+
+    def unpacked(windows_of, from_below, from_above):
+        windows_of = windows_of.reshape(half, 2, 2, frame_count, 2 * model_dim)
         even = windows_of[:, 0, 0] + from_below
         odd = windows_of[:, 1, 1] + from_above
         frames_out = jnp.stack([even, odd], axis=1).reshape(batches, 1, frame_count, 2 * model_dim)
@@ -1499,11 +1501,14 @@
         five = group((0, "f0in"))
         z_three = along_z(spot, [three_next], [g, four.got], TAIL_WORK)
         made = five.first(z_three[:1])
-        last = Second(spot, [four, five], made)
+        home = spread([act, filled(g)])
+        crossed_home = crossing(home)
+        last = Second(spot, [four, five], made + crossed_home)
         z_last = along_z(spot, [last], z_three[1:])
-        home = spread([act, filled(g)])
-        chunks = gathered([[z_early], z_three, z_last], [home])
-        *mats_out, small_out = finish(layers, me, [one, two, three, four, five], chunks, [])
+        chunks_early = gathered([[z_early], z_three], z_last[:1])
+        chunks_late = gathered([z_last], chunks_early[1:])
+        outs = finish(layers, me, [one, two, three], chunks_early, [], chunks_late[:1])
+        *mats_out, small_out = finish(layers, me, [four, five], chunks_late, outs)
         mats_out = [
             v.swapaxes(-1, -2) if turned else v for v, turned in zip(mats_out, (False, True, True, True, False, True))
         ]
@@ -1523,7 +1528,8 @@
             back(l, "a", "f0")
         pieces = None
         home = spread([act, filled(g)])
-    activations, frames_grad = unpacked(home)
+        crossed_home = crossing(home)
+    activations, frames_grad = unpacked(home, *crossed_home)
 
     if not fast:
         mats_out, lines_of = general_sums(layers, members, smalls, order)

time: 366 us -> 375 us (1.025)
  waiting for transfers between devices: 67.7 us -> 76.4 us
    ppermute x1 -> x2, waiting for transfers between devices: 6.06 us -> 18.9 us  [gathered(): one = lax.ppermute(mine, ('rows', 'tm'), along(0))]
    ppermute x3, waiting for transfers between devices: 16 us -> 5.9 us  [first(): self.got = lax.ppermute(sent, ('rows', 'tm'), along(0))]
    ppermute x4, waiting for transfers between devices: 6.98 us -> 13.7 us  [shifted(): return lax.ppermute(array, axis, pairs)]
    ppermute x1 -> x2, waiting for transfers between devices: 7.49 us -> 1.48 us  [gathered(): return [mine, one, two, lax.ppermute(one, ('rows', 'tm'), along(1))]]
    ppermute x6, waiting for transfers between devices: 23.9 us -> 29.2 us  [along_z(): lax.ppermute(v, 'tm', [(i, (i + 2 * k) % 8) for i in range(8)])]
    unnamed x82 -> x83, local copies, waits for them, and re-layouts: 17.2 us -> 20.3 us
    pallas_call x19 -> x20, Pallas kernels: 210 us -> 211 us  [call(): pl.pallas_call(inner, out_shape=[s for s, _ in outs], in_specs=list(ins)...]
  transfers between devices with their start and end apart: 30 -> 33, of which waited for: 15 -> 16; matrix products, arithmetic and copies ran while one was open for 3% -> 2% of each run, Pallas kernels for 34% -> 34%
where the time goes in v2:
time: 375 us; the launch traced here: 370 us
  Pallas kernels  218 us (58%)
  waiting for transfers between devices  76.4 us (20%)
  starting transfers between devices  31.7 us (8%)
  local copies, waits for them, and re-layouts  23.5 us (6%)
  between operations  14.6 us (4%)
    pallas_call x20, Pallas kernels, call(): pl.pallas_call(inner, out_shape=[s for s, _ in outs], in_specs=list(ins)...  211 us
    ppermute x6, waiting for transfers between devices, along_z(): lax.ppermute(v, 'tm', [(i, (i + 2 * k) % 8) for i in range(8)])  29.2 us
    unnamed x83, local copies, waits for them, and re-layouts  20.3 us
    ppermute x2, waiting for transfers between devices, gathered(): one = lax.ppermute(mine, ('rows', 'tm'), along(0))  18.9 us
    ppermute x4, waiting for transfers between devices, shifted(): return lax.ppermute(array, axis, pairs)  13.7 us
    ppermute x4, starting transfers between devices, shifted(): return lax.ppermute(array, axis, pairs)  9.89 us
    ppermute x6, starting transfers between devices, along_z(): lax.ppermute(v, 'tm', [(i, (i + 2 * k) % 8) for i in range(8)])  8.53 us
  transfers between devices with their start and end apart: 33, of which 16 were waited for; matrix products, arithmetic and copies ran while one was open for 2% of the time, Pallas kernels for 34%

profile of v2, /device:TPU:10, one launch (start us, length us, event | category | flops | bytes accessed | tf_op | source)
XLA Modules:
  0.0 369.9 jit_solution(12841540066393649301)
XLA Ops:
  12.7 2.4 collective-permute-start
  16.4 3.2 collective-permute-done.1.refs_4_
  19.5 3.8 %collective-permute-done.refs_3_ = bf16[528,512]{1,0:T(8,128)(2,1)S(1)} collective-permute-done((bf16[528,512]{1,0:T(8,128)(2,1)S(1)}, bf16[528,512]{1,0:T(8,128)(2,1)S(1)}, u32[]{:S(2)}, u32[]{:S(2)}) %collective-permute-start) | collective-permute-done | bytes 540704 | tf_op jit(solution)/shard_map/ppermute | solution.py:37
  24.1 7.5 %pack.1 = (f32[1024,512]{1,0:T(8,128)}, f32[1024,512]{1,0:T(8,128)}, bf16[1024,1024]{1,0:T(8,128)(2,1)}, f32[1024,128]{1,0:T(8,128)}, f32[1024,128]{1,0:T(8,128)...) custom-call(f32[4,128]{1,0:T(4,128)} %get-tuple-element.235.refs_0_, bf16[512,512]{1,0:T(8,128)(2,1)} %bitcast.127, ...), custom_call_target="tpu_custom_call" | custom-call | flops 2147483648 | bytes 12582912 | tf_op jit(solution)/shard_map/pack/pallas_call | solution.py:50
  31.6 42.6 %forward.1 = (bf16[1024,512]{1,0:T(8,128)(2,1)}, f32[2,5,1024,512]{3,2,1,0:T(8,128)}, bf16[2,2,1024,2048]{3,2,1,0:T(8,128)(2,1)}, bf16[2,1024,512]{2,1,0:T(8,128...) custom-call(s32[1]{0:T(128)} %get-tuple-element.93.refs_0_, ...), custom_call_target="tpu_custom_call" | custom-call | flops 15360000000 | bytes 62914560 | tf_op jit(solution)/shard_map/forward/pallas_call | solution.py:50
  74.3 32.4 %back_1_f1_c.1 = (f32[1024,512]{1,0:T(8,128)}, bf16[4,1024,256]{2,1,0:T(8,128)(2,1)}, bf16[4,1024,256]{2,1,0:T(8,128)(2,1)}, f32[8,512]{1,0:T(8,128)}, bf16[4,38...) custom-call(s32[1]{0:T(128)} %get-tuple-element.93.refs_0_, s32[1]{0:T(128)} %bitcast.12.refs_1_, ...), custom_call_target="tpu_custom_call" | custom-call | flops 7381975040 | bytes 16777216 | tf_op jit(solution)/shard_map/back_1_f1_c/pallas_call | solution.py:50
  107.2 5.0 %collective-permute-done.3 = bf16[4,384,256]{2,1,0:T(8,128)(2,1)S(1)} collective-permute-done((bf16[4,384,256]{2,1,0:T(8,128)(2,1)}, bf16[4,384,256]{2,1,0:T(8,128)(2,1)S(1)}, u32[]{:S(2)}, u32[]{:S(2)}) %collective-permute-start.3) | collective-permute-done | bytes 786464 | tf_op jit(solution)/shard_map/ppermute | solution.py:1471
  115.0 2.3 sum_cores.2.refs_18_
  117.3 32.1 %back_1_a_f0.1 = (f32[1024,512]{1,0:T(8,128)}, bf16[4,512,256]{2,1,0:T(8,128)(2,1)}, bf16[4,512,256]{2,1,0:T(8,128)(2,1)}, f32[8,512]{1,0:T(8,128)}, bf16[4,1024...) custom-call(s32[1]{0:T(128)} %get-tuple-element.93.refs_0_, s32[1]{0:T(128)} %bitcast.12.refs_1_, ...), custom_call_target="tpu_custom_call" | custom-call | flops 8053063680 | bytes 16777216 | tf_op jit(solution)/shard_map/back_1_a_f0/pallas_call | solution.py:50
  150.0 20.4 %back_0_f1.1 = (f32[1024,512]{1,0:T(8,128)}, bf16[4,1024,256]{2,1,0:T(8,128)(2,1)}, bf16[4,1024,256]{2,1,0:T(8,128)(2,1)}, f32[8,512]{1,0:T(8,128)}) custom-call(s32[1]{0:T(128)} %get-tuple-element.93.refs_0_, s32[1]{0:T(128)} %bitcast.12.refs_1_, f32[1024,512]{1,0:T(8,128)} %get-tuple-element.114.refs_2_, ...), custom_call_target="tpu_custom_call" | custom-call | flops 5368709120 | bytes 16777216 | tf_op jit(solution)/shard_map/back_0_f1/pallas_call | solution.py:50
  172.1 4.4 %sum_cores.3.refs_15_ = bf16[4,4,384,256]{3,2,1,0:T(8,128)(2,1)} custom-call(bf16[4,4,128,256]{3,2,1,0:T(8,128)(2,1)S(1)} %bitcast.112, bf16[4,4,256,256]{3,2,1,0:T(8,128)(2,1)S(1)} %bitcast.103, bf16[4,4,128,256]{3,2,1,0:T(8,128)(2,1)} %bitcast.19.refs_2_, bf16[4,4,256,256]{3,2,1,0:T(8,128)(2,1)} %bitcast.20.refs_3_, f32[1024,512]{1,0:T(8,128)S(1)} %copy-done.4), custom_call_target="tpu_custom_call" | custom-call | bytes 9437184 | tf_op jit(solution)/shard_map/sum_cores/pallas_call | solution.py:50
  176.7 15.0 %back_0_c.1 = (f32[1024,512]{1,0:T(8,128)}, bf16[4,384,256]{2,1,0:T(8,128)(2,1)}, bf16[4,384,256]{2,1,0:T(8,128)(2,1)}, f32[24,512]{1,0:T(8,128)}) custom-call(s32[1]{0:T(128)} %get-tuple-element.93.refs_0_, s32[1]{0:T(128)} %bitcast.12.refs_1_, f32[1024,512]{1,0:T(8,128)} %get-tuple-element.115.refs_4_.refs_2_, ...), custom_call_target="tpu_custom_call" | custom-call | flops 2013265920 | bytes 16777216 | tf_op jit(solution)/shard_map/back_0_c/pallas_call | solution.py:50
  193.5 3.3 split_first.3
  198.3 25.0 %back_0_a_f0out.1 = (f32[1024,512]{1,0:T(8,128)}, bf16[4,512,256]{2,1,0:T(8,128)(2,1)}, bf16[4,512,256]{2,1,0:T(8,128)(2,1)}, f32[8,512]{1,0:T(8,128)}, bf16[4,5...) custom-call(s32[1]{0:T(128)} %get-tuple-element.93.refs_0_, s32[1]{0:T(128)} %bitcast.12.refs_1_, ...), custom_call_target="tpu_custom_call" | custom-call | flops 4026531840 | bytes 16777216 | tf_op jit(solution)/shard_map/back_0_a_f0out/pallas_call | solution.py:50
  227.5 2.2 collective-permute-done.8
  229.8 2.4 split_first.4
  237.3 13.3 %back_0_f0in.1 = (f32[1024,512]{1,0:T(8,128)}, bf16[4,640,256]{2,1,0:T(8,128)(2,1)}, bf16[4,640,256]{2,1,0:T(8,128)(2,1)}, f32[8,512]{1,0:T(8,128)}) custom-call(s32[1]{0:T(128)} %get-tuple-element.93.refs_0_, s32[1]{0:T(128)} %bitcast.12.refs_1_, f32[1024,512]{1,0:T(8,128)} %get-tuple-element.124.refs_3_.refs_2_, ...), custom_call_target="tpu_custom_call" | custom-call | flops 4026531840 | bytes 16777216 | tf_op jit(solution)/shard_map/back_0_f0in/pallas_call | solution.py:50
  250.7 5.9 %collective-permute-done.13.refs_4_.refs_2_ = bf16[4,2,352,256]{3,2,1,0:T(8,128)(2,1)} collective-permute-done((bf16[4,2,352,256]{3,2,1,0:T(8,128)(2,1)}, bf16[4,2,352,256]{3,2,1,0:T(8,128)(2,1)}, u32[]{:S(2)}, u32[]{:S(2)}) %collective-permute-start.13) | collective-permute-done | bytes 1441824 | tf_op jit(solution)/shard_map/ppermute | solution.py:1223
  261.3 2.4 fusion.4
  268.0 3.6 collective-permute-start.12
  271.7 4.9 %collective-permute-done.11.refs_6_ = bf16[2,128,1024]{2,1,0:T(8,128)(2,1)S(1)} collective-permute-done((bf16[2,128,1024]{2,1,0:T(8,128)(2,1)S(1)}, bf16[2,128,1024]{2,1,0:T(8,128)(2,1)S(1)}, u32[]{:S(2)}, u32[]{:S(2)}) %collective-permute-start.11) | collective-permute-done | bytes 524320 | tf_op jit(solution)/shard_map/ppermute | solution.py:37
  283.7 2.2 collective-permute-start.20
  286.9 7.6 %collective-permute-done.19.refs_4_.refs_3_ = bf16[256,256]{1,0:T(8,128)(2,1)S(1)} collective-permute-done((bf16[256,256]{1,0:T(8,128)(2,1)S(1)}, bf16[256,256]{1,0:T(8,128)(2,1)S(1)}, u32[]{:S(2)}, u32[]{:S(2)}) %collective-permute-start.19) | collective-permute-done | bytes 131104 | tf_op jit(solution)/shard_map/ppermute | solution.py:1289
  298.0 2.1 join.2.refs_1_
  302.1 12.6 %collective-permute-done.24.refs_4_.refs_2_ = bf16[992,256]{1,0:T(8,128)(2,1)} collective-permute-done((bf16[992,256]{1,0:T(8,128)(2,1)}, bf16[992,256]{1,0:T(8,128)(2,1)}, u32[]{:S(2)}, u32[]{:S(2)}) %collective-permute-start.24) | collective-permute-done | bytes 507936 | tf_op jit(solution)/shard_map/ppermute | solution.py:1316
  317.4 2.0 collective-permute-start.23
  320.0 13.8 %collective-permute-done.21.refs_1_ = bf16[512,256]{1,0:T(8,128)(2,1)S(1)} collective-permute-done((bf16[512,256]{1,0:T(8,128)(2,1)S(1)}, bf16[512,256]{1,0:T(8,128)(2,1)S(1)}, u32[]{:S(2)}, u32[]{:S(2)}) %collective-permute-start.21) | collective-permute-done | bytes 262176 | tf_op jit(solution)/shard_map/ppermute | solution.py:1289
  334.4 2.2 collective-permute-done.22.refs_2_
  336.7 2.7 collective-permute-done.23.refs_3_
  344.4 6.3 %collective-permute-done.27.refs_2_ = bf16[512,256]{1,0:T(8,128)(2,1)S(1)} collective-permute-done((bf16[512,256]{1,0:T(8,128)(2,1)}, bf16[512,256]{1,0:T(8,128)(2,1)S(1)}, u32[]{:S(2)}, u32[]{:S(2)}) %collective-permute-start.27) | collective-permute-done | bytes 262176 | tf_op jit(solution)/shard_map/ppermute | solution.py:1316
  352.0 3.7 finish.2
  357.8 2.6 finish.3
  (165 shorter events, 63.5 us)
Async XLA Ops:
  7.2 169.6 %reduce-scatter.10.cloned.1.call-start = ((), (), s32[]{:S(2)}) async-start(), calls=%async_computation.4 | async-start | bytes 3604480
  10.7 8.8 %collective-permute-start.1 = (bf16[528,512]{1,0:T(8,128)(2,1)S(1)}, bf16[528,512]{1,0:T(8,128)(2,1)S(1)}, u32[]{:S(2)}, u32[]{:S(2)}) collective-permute-start(bf16[528,512]{1,0:T(8,128)(2,1)S(1)} %get-tuple-element.232), channel_id=1, source_target_pairs={{1,0},{2,1},{3,2},{4,3},{5,4},{6,5},{7,6},{9,8},{10,9},{11,10},{12... | collective-permute-start | bytes 1622024 | tf_op jit(solution)/shard_map/ppermute | solution.py:37
  12.7 10.7 %collective-permute-start = (bf16[528,512]{1,0:T(8,128)(2,1)S(1)}, bf16[528,512]{1,0:T(8,128)(2,1)S(1)}, u32[]{:S(2)}, u32[]{:S(2)}) collective-permute-start(bf16[528,512]{1,0:T(8,128)(2,1)S(1)} %get-tuple-element.233), channel_id=1, source_target_pairs={{0,1},{1,2},{2,3},{3,4},{4,5},{5,6},{6,7},{8,9},{9,10},{10,11},{11... | collective-permute-start | bytes 1622024 | tf_op jit(solution)/shard_map/ppermute | solution.py:37
  106.7 5.6 %collective-permute-start.2 = (bf16[4,1024,256]{2,1,0:T(8,128)(2,1)}, bf16[4,1024,256]{2,1,0:T(8,128)(2,1)S(1)}, u32[]{:S(2)}, u32[]{:S(2)}) collective-permute-start(bf16[4,1024,256]{2,1,0:T(8,128)(2,1)} %get-tuple-element.112), channel_id=1, source_target_pairs={{0,1},{1,0},{2,3},{3,2},{4,5},{5,4},{6,7},{7,6},{8,9},{9,8},{10,11... | collective-permute-start | bytes 6291464 | tf_op jit(solution)/shard_map/ppermute | solution.py:1471
  106.8 5.5 %collective-permute-start.3 = (bf16[4,384,256]{2,1,0:T(8,128)(2,1)}, bf16[4,384,256]{2,1,0:T(8,128)(2,1)S(1)}, u32[]{:S(2)}, u32[]{:S(2)}) collective-permute-start(bf16[4,384,256]{2,1,0:T(8,128)(2,1)} %get-tuple-element.113), channel_id=1, source_target_pairs={{0,1},{1,0},{2,3},{3,2},{4,5},{5,4},{6,7},{7,6},{8,9},{9,8},{10,11... | collective-permute-start | bytes 2359304 | tf_op jit(solution)/shard_map/ppermute | solution.py:1471
  117.3 117.6 %reduce-scatter.12.cloned.1.call-start = ((), (), s32[]{:S(2)}) async-start(), calls=%async_computation.5 | async-start | bytes 3932160
  149.4 21.0 %collective-permute-start.5 = (bf16[4,1024,256]{2,1,0:T(8,128)(2,1)}, bf16[4,1024,256]{2,1,0:T(8,128)(2,1)}, u32[]{:S(2)}, u32[]{:S(2)}) collective-permute-start(bf16[4,1024,256]{2,1,0:T(8,128)(2,1)} %get-tuple-element.119), channel_id=1, source_target_pairs={{0,1},{1,0},{2,3},{3,2},{4,5},{5,4},{6,7},{7,6},{8,9},{9,8},{10,11... | collective-permute-start | bytes 6291464 | tf_op jit(solution)/shard_map/ppermute | solution.py:1471
  149.5 20.9 %collective-permute-start.4 = (bf16[4,512,256]{2,1,0:T(8,128)(2,1)}, bf16[4,512,256]{2,1,0:T(8,128)(2,1)}, u32[]{:S(2)}, u32[]{:S(2)}) collective-permute-start(bf16[4,512,256]{2,1,0:T(8,128)(2,1)} %get-tuple-element.118), channel_id=1, source_target_pairs={{0,1},{1,0},{2,3},{3,2},{4,5},{5,4},{6,7},{7,6},{8,9},{9,8},{10,11... | collective-permute-start | bytes 3145736 | tf_op jit(solution)/shard_map/ppermute | solution.py:1471
  176.4 121.5 %reduce-scatter.8.cloned.1.call-start = ((), (), s32[]{:S(2)}) async-start(), calls=%async_computation.3 | async-start | bytes 1884160 | tf_op jit(solution)/shard_map/reduce_scatter | solution.py:1267
  176.5 15.2 %collective-permute-start.6 = (bf16[4,1024,256]{2,1,0:T(8,128)(2,1)}, bf16[4,1024,256]{2,1,0:T(8,128)(2,1)}, u32[]{:S(2)}, u32[]{:S(2)}) collective-permute-start(bf16[4,1024,256]{2,1,0:T(8,128)(2,1)} %get-tuple-element.122), channel_id=1, source_target_pairs={{0,1},{1,0},{2,3},{3,2},{4,5},{5,4},{6,7},{7,6},{8,9},{9,8},{10,11... | collective-permute-start | bytes 6291464 | tf_op jit(solution)/shard_map/ppermute | solution.py:1471
  197.8 27.3 %collective-permute-start.7 = (bf16[4,2,256,256]{3,2,1,0:T(8,128)(2,1)}, bf16[4,2,256,256]{3,2,1,0:T(8,128)(2,1)S(1)}, u32[]{:S(2)}, u32[]{:S(2)}) collective-permute-start(bf16[4,2,256,256]{3,2,1,0:T(8,128)(2,1)} %get-tuple-element.132), channel_id=1, source_target_pairs={{0,8},{1,17},{2,10},{3,19},{4,12},{5,21},{6,14},{7,23},{8,0},{9,25... | collective-permute-start | bytes 3145736 | tf_op jit(solution)/shard_map/ppermute | solution.py:1223
  223.3 6.4 %collective-permute-start.9 = (bf16[4,512,256]{2,1,0:T(8,128)(2,1)}, bf16[4,512,256]{2,1,0:T(8,128)(2,1)S(1)}, u32[]{:S(2)}, u32[]{:S(2)}) collective-permute-start(bf16[4,512,256]{2,1,0:T(8,128)(2,1)} %get-tuple-element.138), channel_id=1, source_target_pairs={{0,1},{1,0},{2,3},{3,2},{4,5},{5,4},{6,7},{7,6},{8,9},{9,8},{10,11... | collective-permute-start | bytes 3145736 | tf_op jit(solution)/shard_map/ppermute | solution.py:1471
  224.6 5.1 %collective-permute-start.10 = (bf16[4,512,256]{2,1,0:T(8,128)(2,1)}, bf16[4,512,256]{2,1,0:T(8,128)(2,1)S(1)}, u32[]{:S(2)}, u32[]{:S(2)}) collective-permute-start(bf16[4,512,256]{2,1,0:T(8,128)(2,1)} %get-tuple-element.139), channel_id=1, source_target_pairs={{0,1},{1,0},{2,3},{3,2},{4,5},{5,4},{6,7},{7,6},{8,9},{9,8},{10,11... | collective-permute-start | bytes 3145736 | tf_op jit(solution)/shard_map/ppermute | solution.py:1471
  232.2 24.4 %collective-permute-start.13 = (bf16[4,2,352,256]{3,2,1,0:T(8,128)(2,1)}, bf16[4,2,352,256]{3,2,1,0:T(8,128)(2,1)}, u32[]{:S(2)}, u32[]{:S(2)}) collective-permute-start(bf16[4,2,352,256]{3,2,1,0:T(8,128)(2,1)} %get-tuple-element.142), channel_id=1, source_target_pairs={{0,8},{1,17},{2,10},{3,19},{4,12},{5,21},{6,14},{7,23},{8,0},{9,25... | collective-permute-start | bytes 4325384 | tf_op jit(solution)/shard_map/ppermute | solution.py:1223
  232.9 17.8 %collective-permute-start.15 = (bf16[4,256,256]{2,1,0:T(8,128)(2,1)S(1)}, bf16[4,256,256]{2,1,0:T(8,128)(2,1)}, u32[]{:S(2)}, u32[]{:S(2)}) collective-permute-start(bf16[4,256,256]{2,1,0:T(8,128)(2,1)S(1)} %get-tuple-element.145), channel_id=1, source_target_pairs={{0,16},{1,9},{2,18},{3,11},{4,20},{5,13},{6,22},{7,15},{8,24},{9,1... | collective-permute-start | bytes 1572872 | tf_op jit(solution)/shard_map/ppermute | solution.py:1242
  250.6 13.2 %collective-permute-start.14 = (bf16[4,640,256]{2,1,0:T(8,128)(2,1)}, bf16[4,640,256]{2,1,0:T(8,128)(2,1)S(1)}, u32[]{:S(2)}, u32[]{:S(2)}) collective-permute-start(bf16[4,640,256]{2,1,0:T(8,128)(2,1)} %get-tuple-element.144), channel_id=1, source_target_pairs={{0,1},{1,0},{2,3},{3,2},{4,5},{5,4},{6,7},{7,6},{8,9},{9,8},{10,11... | collective-permute-start | bytes 3932168 | tf_op jit(solution)/shard_map/ppermute | solution.py:1471
  264.7 13.7 %collective-permute-start.16 = (bf16[4,2,160,256]{3,2,1,0:T(8,128)(2,1)S(1)}, bf16[4,2,160,256]{3,2,1,0:T(8,128)(2,1)S(1)}, u32[]{:S(2)}, u32[]{:S(2)}) collective-permute-start(bf16[4,2,160,256]{3,2,1,0:T(8,128)(2,1)S(1)} %get-tuple-element.148), channel_id=1, source_target_pairs={{0,8},{1,17},{2,10},{3,19},{4,12},{5,21},{6,14},{7,23},{8,0},{9,25... | collective-permute-start | bytes 1966088 | tf_op jit(solution)/shard_map/ppermute | solution.py:1223
  266.1 10.5 %collective-permute-start.11 = (bf16[2,128,1024]{2,1,0:T(8,128)(2,1)S(1)}, bf16[2,128,1024]{2,1,0:T(8,128)(2,1)S(1)}, u32[]{:S(2)}, u32[]{:S(2)}) collective-permute-start(bf16[2,128,1024]{2,1,0:T(8,128)(2,1)S(1)} %get-tuple-element.210), channel_id=1, source_target_pairs={{0,1},{1,2},{2,3},{3,4},{4,5},{5,6},{6,7},{8,9},{9,10},{10,11},{11... | collective-permute-start | bytes 1572872 | tf_op jit(solution)/shard_map/ppermute | solution.py:37
  268.0 10.3 %collective-permute-start.12 = (bf16[2,128,1024]{2,1,0:T(8,128)(2,1)S(1)}, bf16[2,128,1024]{2,1,0:T(8,128)(2,1)S(1)}, u32[]{:S(2)}, u32[]{:S(2)}) collective-permute-start(bf16[2,128,1024]{2,1,0:T(8,128)(2,1)S(1)} %get-tuple-element.211), channel_id=1, source_target_pairs={{1,0},{2,1},{3,2},{4,3},{5,4},{6,5},{7,6},{9,8},{10,9},{11,10},{12... | collective-permute-start | bytes 1572872 | tf_op jit(solution)/shard_map/ppermute | solution.py:37
  280.3 16.2 %collective-permute-start.17 = (bf16[4,512,256]{2,1,0:T(8,128)(2,1)S(1)}, bf16[4,512,256]{2,1,0:T(8,128)(2,1)S(1)}, u32[]{:S(2)}, u32[]{:S(2)}) collective-permute-start(bf16[4,512,256]{2,1,0:T(8,128)(2,1)S(1)} %get-tuple-element.150), channel_id=1, source_target_pairs={{0,16},{1,9},{2,18},{3,11},{4,20},{5,13},{6,22},{7,15},{8,24},{9,1... | collective-permute-start | bytes 3145736 | tf_op jit(solution)/shard_map/ppermute | solution.py:1242
  281.1 5.8 %collective-permute-start.18 = (bf16[256,256]{1,0:T(8,128)(2,1)S(1)}, bf16[256,256]{1,0:T(8,128)(2,1)S(1)}, u32[]{:S(2)}, u32[]{:S(2)}) collective-permute-start(bf16[256,256]{1,0:T(8,128)(2,1)S(1)} %get-tuple-element.151), channel_id=1, source_target_pairs={{0,2},{1,3},{2,4},{3,5},{4,6},{5,7},{6,0},{7,1},{8,10},{9,11},{10,... | collective-permute-start | bytes 393224 | tf_op jit(solution)/shard_map/ppermute | solution.py:1289
  282.7 11.8 %collective-permute-start.19 = (bf16[256,256]{1,0:T(8,128)(2,1)S(1)}, bf16[256,256]{1,0:T(8,128)(2,1)S(1)}, u32[]{:S(2)}, u32[]{:S(2)}) collective-permute-start(bf16[256,256]{1,0:T(8,128)(2,1)S(1)} %get-tuple-element.152), channel_id=1, source_target_pairs={{0,4},{1,5},{2,6},{3,7},{4,0},{5,1},{6,2},{7,3},{8,12},{9,13},{10,... | collective-permute-start | bytes 393224 | tf_op jit(solution)/shard_map/ppermute | solution.py:1289
  283.7 12.7 %collective-permute-start.20 = (bf16[256,256]{1,0:T(8,128)(2,1)S(1)}, bf16[256,256]{1,0:T(8,128)(2,1)S(1)}, u32[]{:S(2)}, u32[]{:S(2)}) collective-permute-start(bf16[256,256]{1,0:T(8,128)(2,1)S(1)} %get-tuple-element.153), channel_id=1, source_target_pairs={{0,6},{1,7},{2,0},{3,1},{4,2},{5,3},{6,4},{7,5},{8,14},{9,15},{10,... | collective-permute-start | bytes 393224 | tf_op jit(solution)/shard_map/ppermute | solution.py:1289
  300.1 14.6 %collective-permute-start.24 = (bf16[992,256]{1,0:T(8,128)(2,1)}, bf16[992,256]{1,0:T(8,128)(2,1)}, u32[]{:S(2)}, u32[]{:S(2)}) collective-permute-start(bf16[992,256]{1,0:T(8,128)(2,1)} %join.2.refs_1_), channel_id=1, source_target_pairs={{0,8},{1,17},{2,10},{3,19},{4,12},{5,21},{6,14},{7,23},{8,0},{9,25... | collective-permute-start | bytes 1523720 | tf_op jit(solution)/shard_map/ppermute | solution.py:1316
  301.4 38.0 %collective-permute-start.25 = (bf16[992,256]{1,0:T(8,128)(2,1)}, bf16[992,256]{1,0:T(8,128)(2,1)}, u32[]{:S(2)}, u32[]{:S(2)}) collective-permute-start(bf16[992,256]{1,0:T(8,128)(2,1)} %join.2.refs_1_), channel_id=1, source_target_pairs={{0,16},{1,9},{2,18},{3,11},{4,20},{5,13},{6,22},{7,15},{8,24},{9,1... | collective-permute-start | bytes 1523720 | tf_op jit(solution)/shard_map/ppermute | solution.py:1317
  314.6 24.7 %collective-permute-start.26 = (bf16[992,256]{1,0:T(8,128)(2,1)}, bf16[992,256]{1,0:T(8,128)(2,1)}, u32[]{:S(2)}, u32[]{:S(2)}) collective-permute-start(bf16[992,256]{1,0:T(8,128)(2,1)} %collective-permute-done.24.refs_4_.refs_2_), channel_id=1, source_target_pairs={{0,16},{1,9},{2,18},{3,11},{4,20},{5,13},{6,22},{7,15},{8,24},{9,1... | collective-permute-start | bytes 1523720 | tf_op jit(solution)/shard_map/ppermute | solution.py:1318
  315.7 18.0 %collective-permute-start.21 = (bf16[512,256]{1,0:T(8,128)(2,1)S(1)}, bf16[512,256]{1,0:T(8,128)(2,1)S(1)}, u32[]{:S(2)}, u32[]{:S(2)}) collective-permute-start(bf16[512,256]{1,0:T(8,128)(2,1)S(1)} %get-tuple-element.155), channel_id=1, source_target_pairs={{0,2},{1,3},{2,4},{3,5},{4,6},{5,7},{6,0},{7,1},{8,10},{9,11},{10,... | collective-permute-start | bytes 786440 | tf_op jit(solution)/shard_map/ppermute | solution.py:1289
  315.7 20.9 %collective-permute-start.22 = (bf16[512,256]{1,0:T(8,128)(2,1)S(1)}, bf16[512,256]{1,0:T(8,128)(2,1)}, u32[]{:S(2)}, u32[]{:S(2)}) collective-permute-start(bf16[512,256]{1,0:T(8,128)(2,1)S(1)} %get-tuple-element.156), channel_id=1, source_target_pairs={{0,4},{1,5},{2,6},{3,7},{4,0},{5,1},{6,2},{7,3},{8,12},{9,13},{10,... | collective-permute-start | bytes 786440 | tf_op jit(solution)/shard_map/ppermute | solution.py:1289
  317.4 22.0 %collective-permute-start.23 = (bf16[512,256]{1,0:T(8,128)(2,1)S(1)}, bf16[512,256]{1,0:T(8,128)(2,1)}, u32[]{:S(2)}, u32[]{:S(2)}) collective-permute-start(bf16[512,256]{1,0:T(8,128)(2,1)S(1)} %get-tuple-element.157), channel_id=1, source_target_pairs={{0,6},{1,7},{2,0},{3,1},{4,2},{5,3},{6,4},{7,5},{8,14},{9,15},{10,... | collective-permute-start | bytes 786440 | tf_op jit(solution)/shard_map/ppermute | solution.py:1289
  341.4 9.4 %collective-permute-start.27 = (bf16[512,256]{1,0:T(8,128)(2,1)}, bf16[512,256]{1,0:T(8,128)(2,1)S(1)}, u32[]{:S(2)}, u32[]{:S(2)}) collective-permute-start(bf16[512,256]{1,0:T(8,128)(2,1)} %join.3.refs_5_.refs_1_), channel_id=1, source_target_pairs={{0,8},{1,17},{2,10},{3,19},{4,12},{5,21},{6,14},{7,23},{8,0},{9,25... | collective-permute-start | bytes 786440 | tf_op jit(solution)/shard_map/ppermute | solution.py:1316
  343.2 12.4 %collective-permute-start.28 = (bf16[512,256]{1,0:T(8,128)(2,1)S(1)}, bf16[512,256]{1,0:T(8,128)(2,1)S(1)}, u32[]{:S(2)}, u32[]{:S(2)}) collective-permute-start(bf16[512,256]{1,0:T(8,128)(2,1)S(1)} %copy-done.26), channel_id=1, source_target_pairs={{0,16},{1,9},{2,18},{3,11},{4,20},{5,13},{6,22},{7,15},{8,24},{9,1... | collective-permute-start | bytes 786440 | tf_op jit(solution)/shard_map/ppermute | solution.py:1317
  350.8 6.4 %collective-permute-start.29 = (bf16[512,256]{1,0:T(8,128)(2,1)S(1)}, bf16[512,256]{1,0:T(8,128)(2,1)S(1)}, u32[]{:S(2)}, u32[]{:S(2)}) collective-permute-start(bf16[512,256]{1,0:T(8,128)(2,1)S(1)} %collective-permute-done.27.refs_2_), channel_id=1, source_target_pairs={{0,16},{1,9},{2,18},{3,11},{4,20},{5,13},{6,22},{7,15},{8,24},{9,1... | collective-permute-start | bytes 786440 | tf_op jit(solution)/shard_map/ppermute | solution.py:1318
  (40 other events, 221.9 us)
Sparse Core Ops, SparseCore 0:
  117.4 42.8 reduce-scatter.9
  176.6 47.7 reduce-scatter.11
  237.4 32.8 reduce-scatter.7
